TPU v7x, 32 devices: a whole 2x2x4 slice. The times are simulated.
32 devices in a mesh: section: 2 (over y), fsdp: 4 (over z), dp: 4 (over x, core).
Axes of the slice: x: 2, y: 2, z: 4, core: 2. Of those that a mesh axis runs over, the one named last changes fastest.
Arguments:
- inputs: bfloat16 [2, 4, 1024, 1536], P(None, 'dp', 'fsdp'), may hold values from -6 to 6
- segment: int32 [2, 4, 1024], P(None, 'dp', 'fsdp'), may hold values from 0 to 2, as said below
- cotangent: bfloat16 [2, 4, 1024, 1536], P(None, 'dp', 'fsdp'), may hold values from -6 to 6
- norm_gain: float32 [2, 1, 1536], P('section'), may hold values from 0.5 to 1.5
- in_weight: bfloat16 [2, 1, 1536, 6448], P('section', None, 'fsdp'), may hold values from -0.15625 to 0.15625
- conv_weight: float32 [2, 1, 4, 3328], P('section'), may hold values from -3 to 3
- conv_bias: float32 [2, 1, 3328], P('section'), may hold values from -3 to 3
- dt_bias: float32 [2, 1, 48], P('section'), may hold values from -7 to -2
- a_log: float32 [2, 1, 48], P('section'), may hold values from -4 to 1
- d_skip: float32 [2, 1, 48], P('section'), may hold values from 0.5 to 1.5
- gate_gain: float32 [2, 1, 3072], P('section'), may hold values from 0.5 to 1.5
- out_weight: bfloat16 [2, 1, 3072, 1536], P('section', None, 'fsdp'), may hold values from -0.109375 to 0.109375
Outputs:
- final: bfloat16 [2, 4, 1024, 1536], P('section', 'dp', 'fsdp')
- input_grad: bfloat16 [2, 4, 1024, 1536], P('section', 'dp', 'fsdp')
- norm_gain_grad: float32 [2, 1, 1536], P('section')
- in_weight_grad: float32 [2, 1, 1536, 6448], P('section', None, 'fsdp')
- conv_weight_grad: float32 [2, 1, 4, 3328], P('section')
- conv_bias_grad: float32 [2, 1, 3328], P('section')
- dt_bias_grad: float32 [2, 1, 48], P('section')
- a_log_grad: float32 [2, 1, 48], P('section')
- d_skip_grad: float32 [2, 1, 48], P('section')
- gate_gain_grad: float32 [2, 1, 3072], P('section')
- out_weight_grad: float32 [2, 1, 3072, 1536], P('section', None, 'fsdp')
Inputs may be any that keep to these rules, and one draw needn't show every extreme that they name: Along each sequence the segment numbers never fall; they start at 0 and end at 2, and segment 1 starts among the first 256 tokens and ends among the last 256.
All inputs are finite; a program needn't handle non-finite values.
Results may differ from a plain program's by a relative error of at most 0.01575.
The roundings to bfloat16 on the way count: a program that leaves them out, or rounds other values in their place, can miss the bound.
Values may be sent and summed in bfloat16 or wider, within the bound.
A program may use at most 384 MiB of HBM per device.

v0:
```python
import functools

import jax
import jax.numpy as jnp
from jax import lax
from jax.experimental import pallas as pl
from jax.experimental.pallas import tpu as pltpu
from jax.sharding import PartitionSpec as P

D = 1536
H = 48
P_SIZE = 64
N = 128
K = 4
DI = 3072
DC = 3328
DIN = 6448
EPSILON = 1e-05
HIGHEST = lax.Precision.HIGHEST
BF16 = jnp.bfloat16
F32 = jnp.float32
Q = 128
LANES = 128


def dot(a, b, dims=((1,), (0,)), precision=None):
    return lax.dot_general(a, b, (dims, ((), ())), preferred_element_type=F32, precision=precision)


def low_dot(a, b, dims=((1,), (0,))):
    return dot(a.astype(BF16), b.astype(BF16), dims)


def fine_dot(a, b, dims=((1,), (0,))):
    return dot(a, b, dims, HIGHEST)


def halves(value):
    high = value.astype(BF16)
    return high, (value - high.astype(F32)).astype(BF16)


def split_dot(a, b, dims=((1,), (0,))):
    (a_high, a_low), (b_high, b_low) = halves(a), halves(b)
    a_axis, b_axis = dims[0][0], dims[1][0]
    both = dot(
        jnp.concatenate([a_high, a_low], axis=a_axis), jnp.concatenate([b_high, b_high], axis=b_axis), dims
    )
    return both + dot(a_high, b_low, dims)


def pair_lanes(table, first, low_half):
    return jnp.where(low_half, table[:, first : first + 1], table[:, first + 1 : first + 2])


def decay_tables(proj_dt, dt_bias, a_row, tri):
    shifted = proj_dt + dt_bias
    step = jnp.maximum(shifted, 0.0) + jnp.log1p(jnp.exp(-jnp.abs(shifted)))
    log_decay = -step * jnp.exp(a_row)
    cumulative = fine_dot(tri, log_decay)
    return shifted, step, log_decay, cumulative


def triangles():
    row = lax.broadcasted_iota(jnp.int32, (Q, Q), 0)
    column = lax.broadcasted_iota(jnp.int32, (Q, Q), 1)
    return row, column


MESH_ID = pl.DeviceIdType.MESH
VMEM_LIMIT = 60 * 1024 * 1024


def remote(src, dst, send_sem, recv_sem, device):
    return pltpu.make_async_remote_copy(
        src_ref=src, dst_ref=dst, send_sem=send_sem, recv_sem=recv_sem, device_id=device, device_id_type=MESH_ID
    )


def greet(devices):
    barrier = pltpu.get_barrier_semaphore()
    count = 0
    for condition, device in devices:
        if condition is None:
            pl.semaphore_signal(barrier, inc=1, device_id=device, device_id_type=MESH_ID)
            count = count + 1
        else:

            @pl.when(condition)
            def _():
                pl.semaphore_signal(barrier, inc=1, device_id=device, device_id_type=MESH_ID)

            count = count + condition.astype(jnp.int32)
    pl.semaphore_wait(barrier, count)


def bits_of(peers):
    return [1 << k for k in range(peers.bit_length() - 1)]


def has_bit(value, bit):
    return (value // bit) % 2


def flip(value, bits):
    bit = 1
    out = value
    while bit <= bits:
        if bits & bit:
            out = out + bit * (1 - 2 * has_bit(value, bit))
        bit = bit * 2
    return out


def to_column(row):
    down, across = triangles()
    return jnp.sum(jnp.where(down == across, jnp.broadcast_to(row, (Q, Q)), 0.0), axis=1, keepdims=True)


def to_row(column, offset=0):
    shape = (column.shape[0], Q)
    down = lax.broadcasted_iota(jnp.int32, shape, 0)
    across = lax.broadcasted_iota(jnp.int32, shape, 1)
    return jnp.sum(jnp.where(across == down + offset, jnp.broadcast_to(column, shape), 0.0), axis=0, keepdims=True)


class GroupTiles:

    def __init__(self, tiles, send_sem, recv_sem, here, peers):
        self.tiles, self.send_sem, self.recv_sem, self.here, self.peers = tiles, send_sem, recv_sem, here, peers

    def copies(self):
        return [
            remote(
                self.tiles.at[0], self.tiles.at[j], self.send_sem.at[j], self.recv_sem.at[j],
                {"dp": flip(self.here, j)},
            )
            for j in range(1, self.peers)
        ]

    def begin(self):
        for copy in self.copies():
            copy.start()

    def finish(self):
        for copy in self.copies():
            copy.wait()
        total = self.tiles[0]
        for j in range(1, self.peers):
            total = total + self.tiles[j]
        return total


def group_tiles(tiles, send_sem, recv_sem, here, peers):
    group = GroupTiles(tiles, send_sem, recv_sem, here, peers)
    group.begin()
    return group.finish()


class GroupRows:

    def __init__(self, where, here, peers, send_sem, recv_sem):
        self.where, self.here, self.peers = where, here, peers
        self.send_sem, self.recv_sem = send_sem, recv_sem

    def part(self, j):
        return self.where(flip(self.here, j))

    def copy(self, j, bit, source=None):
        part = self.part(j)
        return remote(
            part if source is None else source, part, self.send_sem.at[j ^ bit], self.recv_sem.at[j ^ bit],
            {"dp": flip(self.here, bit)},
        )

    def begin(self, source=None):
        for bit in bits_of(self.peers)[::-1]:
            self.copy(0, bit, source).start()

    def phase(self, bit):
        for j in range(bit, self.peers, 2 * bit):
            self.copy(j ^ bit, bit).wait_send()
            landing = self.part(j)
            remote(
                landing, landing, self.send_sem.at[j], self.recv_sem.at[j], {"dp": flip(self.here, bit)}
            ).wait_recv()
            for lower in bits_of(bit)[::-1]:
                self.copy(j, lower).start()

    def relay(self):
        for bit in bits_of(self.peers)[:0:-1]:
            self.phase(bit)

    def close(self):
        self.phase(1)

    def finish(self):
        self.relay()
        self.close()


def rows_of(whole, rows):
    return lambda device: whole.at[pl.ds(pl.multiple_of(device * rows, 8), rows)]


def rms_parts(values):
    return lax.rsqrt(jnp.mean(values * values, axis=-1, keepdims=True) + EPSILON)


class BlockSum:

    def __init__(self, partial, landed, here, peers, send_sem, recv_sem):
        self.partial, self.landed, self.here, self.peers = partial, landed, here, peers
        self.bits = bits_of(peers)
        self.send_sem, self.recv_sem = send_sem, recv_sem

    def copy(self, k, block, owner):
        return remote(
            self.partial.at[block, owner], self.landed.at[k, block, owner // 2], self.send_sem.at[k, block, owner],
            self.recv_sem.at[k, block, owner], {"dp": flip(self.here, self.bits[k])},
        )

    def total(self, block, owner, stages):
        total = self.partial[block, owner].astype(F32)
        for m in range(stages):
            self.copy(m, block, owner).wait_recv()
            total = total + self.landed[m, block, owner // 2].astype(F32)
        return total

    def leaving(self, k):
        return [flip(self.here, j) for j in range(self.bits[k], self.peers, 2 * self.bits[k])]

    def send(self, k, block):
        for owner in self.leaving(k):
            if k > 0:
                self.partial[block, owner] = self.total(block, owner, k).astype(self.partial.dtype)
            self.copy(k, block, owner).start()

    def own(self, block):
        return self.total(block, self.here, len(self.bits))

    def settle(self, blocks):
        for block in range(blocks):
            for k in range(len(self.bits)):
                for owner in self.leaving(k):
                    self.copy(k, block, owner).wait_send()


class Deal:

    def __init__(self, chunk, own, nf, nd, z, d, send_sem, recv_sem, outward):
        self.chunk, self.own, self.nf, self.nd, self.z, self.d = chunk, own, nf, nd, z, d
        self.send_sem, self.recv_sem, self.outward = send_sem, recv_sem, outward
        self.rows = chunk.shape[0] // nd

    def part(self, o):
        return self.chunk.at[pl.ds(pl.multiple_of(o * self.rows, 16), self.rows)]

    def holder(self, b):
        return {"fsdp": b, "dp": self.z}

    def worker(self, o):
        return {"fsdp": self.d, "dp": o}

    def at_home(self, k):
        return (self.z == self.d) & (self.z == k)

    def send(self, k):
        if self.outward:
            return remote(
                self.own.at[k], self.part(self.d), self.send_sem.at[k], self.recv_sem.at[self.d], self.holder(k)
            )
        return remote(
            self.part(k), self.own.at[self.z], self.send_sem.at[k], self.recv_sem.at[self.z], self.worker(k)
        )

    def recv(self, k):
        if self.outward:
            part = self.part(k)
            return remote(part, part, self.send_sem.at[k], self.recv_sem.at[k], self.worker(k))
        part = self.own.at[k]
        return remote(part, part, self.send_sem.at[k], self.recv_sem.at[k], self.holder(k))

    def keep(self, k):
        if self.outward:
            return pltpu.make_async_copy(self.own.at[k], self.part(k), self.send_sem.at[k])
        return pltpu.make_async_copy(self.part(k), self.own.at[k], self.send_sem.at[k])

    def start(self, k):
        @pl.when(self.at_home(k))
        def _():
            self.keep(k).start()

        @pl.when(jnp.logical_not(self.at_home(k)))
        def _():
            self.send(k).start()

    def start_all(self):
        for k in range(self.nf):
            self.start(k)

    def arrive(self):
        for k in range(self.nf):

            @pl.when(self.at_home(k))
            def _():
                self.keep(k).wait()

            @pl.when(jnp.logical_not(self.at_home(k)))
            def _():
                self.recv(k).wait_recv()

    def settle(self):
        for k in range(self.nf):

            @pl.when(jnp.logical_not(self.at_home(k)))
            def _():
                self.send(k).wait_send()


def deal_partners(nf, nd, z, d):
    out = []
    for k in range(nf):
        elsewhere = (z != d) | (z != k)
        out += [(elsewhere, {"fsdp": k, "dp": z}), (elsewhere, {"fsdp": d, "dp": k})]
    return out


class SectionGather:

    def __init__(self, held, section, nf, y, z, sems, own=None):
        self.own = own
        self.held, self.section, self.nf, self.y, self.z, self.sems = held, section, nf, y, z, sems
        width = held.shape[1]
        first = -(-width // 32) * 16
        self.spans = [(0, first), (first, width - first)]
        self.peer = {"section": 1 - y}

    def block(self, b, part):
        start, size = self.spans[part]
        return self.held.at[b, pl.ds(start, size)]

    def each(self, body):
        for part in range(2):
            owner = self.y == self.section

            @pl.when(owner if part == 0 else jnp.logical_not(owner))
            def _():
                body(part)

    def own_part(self, part):
        start, size = self.spans[part]
        return self.own.at[pl.ds(start, size)]

    def send(self, b, part, row, k, landed, device, source=None):
        here = self.block(b, part)
        return remote(
            here if source is None else source, here, self.sems.at[row, k], self.sems.at[landed, k], device
        )

    def right(self, k, b, part, source=None):
        return self.send(b, part, 0, k, 2, {"fsdp": self.z + 1}, source)

    def left(self, k, b, part, source=None):
        return self.send(b, part, 1, k, 3, {"fsdp": self.z - 1}, source)

    def over(self, k, b, part, source=None):
        return self.send(b, part, 4, k, 5, self.peer, source)

    def cross(self):
        here = self.block(self.z, 1)
        return remote(self.own_part(1), here, self.sems.at[6, 0], self.sems.at[6, 1], self.peer)

    def keep(self):
        return pltpu.make_async_copy(self.own, self.held.at[self.z], self.sems.at[6, 2])

    def has_right(self):
        return self.z < self.nf - 1

    def has_left(self):
        return self.z > 0

    def start_cross(self):
        @pl.when(self.y == self.section)
        def _():
            self.cross().start()
            self.keep().start()

    def begin(self):
        def body(part):
            source = None
            if part == 1:
                self.cross().wait_recv()
            else:
                source = self.own_part(0)

            @pl.when(self.has_right())
            def _():
                self.right(1, self.z, part, source).start()

            @pl.when(self.has_left())
            def _():
                self.left(1, self.z, part, source).start()

            if part == 0:
                self.cross().wait_send()
                self.over(0, self.z, 0, source).start()

        self.each(body)

    def settle_begin(self):
        def body(part):
            @pl.when(self.has_right())
            def _():
                self.right(1, self.z, part).wait_send()

            @pl.when(self.has_left())
            def _():
                self.left(1, self.z, part).wait_send()

            if part == 0:
                self.over(0, self.z, 0).wait_send()
                self.keep().wait()
            else:
                self.over(0, self.z, 0).wait_recv()

        self.each(body)

    def sides(self, k, body):
        @pl.when(self.z >= k)
        def _():
            body(self.z - k, k, True)

        @pl.when(self.z + k < self.nf)
        def _():
            body(self.z + k, self.nf + k, False)

    def arrive(self, k):
        def body(part):
            def one(b, index, from_left):
                if from_left:
                    self.right(k, b, part).wait_recv()
                else:
                    self.left(k, b, part).wait_recv()

            self.sides(k, one)

        self.each(body)

    def relay(self, k):
        def body(part):
            def one(b, index, from_left):
                if k < self.nf - 1:
                    if from_left:

                        @pl.when(self.has_right())
                        def _():
                            self.right(k + 1, b, part).start()

                    else:

                        @pl.when(self.has_left())
                        def _():
                            self.left(k + 1, b, part).start()

                self.over(index, b, part).start()

            self.sides(k, one)

        self.each(body)

    def settle(self, k):
        def body(part):
            def one(b, index, from_left):
                self.over(index, b, part).wait_send()
                self.over(index, b, 1 - part).wait_recv()
                if k < self.nf - 1:
                    if from_left:

                        @pl.when(self.has_right())
                        def _():
                            self.right(k + 1, b, part).wait_send()

                    else:

                        @pl.when(self.has_left())
                        def _():
                            self.left(k + 1, b, part).wait_send()

            self.sides(k, one)

        self.each(body)


class OutGather:

    def __init__(self, source, held, section, nf, y, z, d, sems, staged):
        self.staged = staged
        self.source, self.held, self.section, self.nf = source, held, section, nf
        self.y, self.z, self.d, self.sems = y, z, d, sems
        self.pieces = sems.shape[1]
        self.rows = source.shape[0] // self.pieces
        self.columns = source.shape[1] // 2
        self.peer = {"section": 1 - y}
        self.source_here = z == d

    def owner(self):
        return self.y == self.section

    def piece(self, ref, part, i):
        return ref.at[pl.ds(i * self.rows, self.rows), pl.ds(part * self.columns, self.columns)]

    def send(self, i, part, row, landed, device, source=None):
        target = self.piece(self.held, part, i)
        return remote(
            target if source is None else self.piece(source, part, i), target, self.sems.at[row, i],
            self.sems.at[landed, i], device,
        )

    def right(self, i, part, source=None):
        return self.send(i, part, 0, 2, {"fsdp": self.z + 1}, source)

    def left(self, i, part, source=None):
        return self.send(i, part, 1, 2, {"fsdp": self.z - 1}, source)

    def over(self, i, part, source=None):
        return self.send(i, part, 3, 4, self.peer, source)

    def cross(self):
        columns = pl.ds(self.columns, self.columns)
        return remote(
            self.source.at[:, columns], self.held.at[:, columns], self.sems.at[5, 0], self.sems.at[5, 1], self.peer
        )

    def stage(self):
        return pltpu.make_async_copy(self.source, self.staged, self.sems.at[5, 2])

    def keep(self):
        return pltpu.make_async_copy(self.staged, self.held, self.sems.at[5, 3])

    def goes_right(self):
        return (self.z >= self.d) & (self.z < self.nf - 1)

    def goes_left(self):
        return (self.z <= self.d) & (self.z > 0)

    def each(self, condition, body):
        for part in range(2):
            mine = self.owner() if part == 0 else jnp.logical_not(self.owner())

            @pl.when(condition & mine)
            def _():
                body(part)

    def along(self, i, part, action, source=None):
        @pl.when(self.goes_right())
        def _():
            action(self.right(i, part, source))

        @pl.when(self.goes_left())
        def _():
            action(self.left(i, part, source))

    def begin(self):
        @pl.when(self.source_here & self.owner())
        def _():
            self.cross().start()
            self.stage().start()
            for i in range(self.pieces):
                self.along(i, 0, lambda copy: copy.start(), self.source)

    def begin_other(self):
        @pl.when(self.source_here & jnp.logical_not(self.owner()))
        def _():
            self.cross().wait_recv()
            for i in range(self.pieces):
                self.along(i, 1, lambda copy: copy.start())

    def hops(self, distance):
        def body(part):
            for i in range(self.pieces):
                self.right(i, part).wait_recv()
                self.along(i, part, lambda copy: copy.start())

        self.each((self.z == self.d + distance) | (self.z == self.d - distance), body)

    def hand_over(self):
        @pl.when(self.source_here & self.owner())
        def _():
            self.stage().wait()
            self.keep().start()
            for i in range(self.pieces):
                self.over(i, 0, self.source).start()

        def body(part):
            for i in range(self.pieces):
                self.over(i, part).start()

        self.each(jnp.logical_not(self.source_here), body)

    def settle(self):
        @pl.when(self.source_here & self.owner())
        def _():
            self.cross().wait_send()
            self.keep().wait()

        def at_source(part):
            for i in range(self.pieces):
                self.along(i, part, lambda copy: copy.wait_send())
                if part == 0:
                    self.over(i, 0).wait_send()
                else:
                    self.over(i, 0).wait_recv()

        def elsewhere(part):
            for i in range(self.pieces):
                self.along(i, part, lambda copy: copy.wait_send())
                self.over(i, part).wait_send()
                self.over(i, 1 - part).wait_recv()

        self.each(self.source_here, at_source)
        self.each(jnp.logical_not(self.source_here), elsewhere)


def line_neighbours(nf, y, z):
    return [
        (None, {"section": 1 - y}),
        (z < nf - 1, {"fsdp": z + 1}),
        (z > 0, {"fsdp": z - 1}),
    ]


class SectionSum:

    def __init__(self, view, nf, y, z, own, landed, chain, sems, result):
        self.view, self.nf, self.y, self.z, self.result = view, nf, y, z, result
        self.own, self.landed, self.chain = own, landed, chain
        self.load_sem, self.over_send, self.over_recv, self.chain_send, self.chain_recv = (
            sems.at[0], sems.at[1], sems.at[2], sems.at[3], sems.at[4]
        )
        self.part_rows = own.shape[1]

    def load(self, block):
        return pltpu.make_async_copy(self.view(block, self.y), self.own.at[block], self.load_sem.at[block])

    def over(self, block):
        return remote(
            self.view(block, 1 - self.y), self.landed.at[block], self.over_send.at[block], self.over_recv.at[block],
            {"section": 1 - self.y},
        )

    def right(self, block):
        return remote(
            self.own.at[block], self.chain.at[block], self.chain_send.at[block], self.chain_recv.at[block],
            {"fsdp": self.z + 1},
        )

    def left(self, block, arrives):
        slot = self.nf if arrives else block
        return remote(
            self.own.at[block], self.chain.at[slot], self.chain_send.at[block], self.chain_recv.at[slot],
            {"fsdp": self.z - 1},
        )

    def at(self, k, body):
        if k == 0:
            body(self.z, False)
            return

        @pl.when(self.z + k < self.nf)
        def _():
            body(self.z + k, True)

        @pl.when(self.z - k >= 0)
        def _():
            body(self.z - k, False)

    def begin(self):
        self.at(self.nf - 1, lambda block, rightward: self.over(block).start())
        for k in range(self.nf - 1, -1, -1):
            self.at(k, lambda block, rightward: self.load(block).start())

    def add(self, block, sources, target):
        step = 32

        def some(i, carry):
            rows = pl.ds(pl.multiple_of(i * step, 16), step)
            total = self.own[block, rows, :].astype(F32)
            for ref, slot in sources:
                total = total + ref[slot, rows, :].astype(F32)
            if target is None:
                self.own[block, rows, :] = total.astype(BF16)
            else:
                target[rows, :] = total.astype(BF16)
            return carry

        lax.fori_loop(0, self.part_rows // step, some, 0)

    def ready(self, block):
        self.load(block).wait()
        self.over(block).wait_recv()

    def stage(self, k):
        z, nf = self.z, self.nf
        self.at(k, lambda block, rightward: self.ready(block))
        self.at(k - 1, lambda block, rightward: self.over(block).start())

        def one(block, rightward):
            far_end = z == 0 if rightward else z == nf - 1
            arrived = self.right(block) if rightward else self.left(block, False)
            leaving = self.right(block) if rightward else self.left(block, k == 1)

            @pl.when(jnp.logical_not(far_end))
            def _():
                arrived.wait_recv()
                self.add(block, [(self.landed, block), (self.chain, block)], None)

            @pl.when(far_end)
            def _():
                self.add(block, [(self.landed, block)], None)

            leaving.start()

        self.at(k, one)

    def finish(self):
        z, nf, target = self.z, self.nf, self.result
        self.ready(z)

        @pl.when(z > 0)
        def _():
            self.right(z).wait_recv()

        @pl.when(z < nf - 1)
        def _():
            self.left(z, True).wait_recv()

        @pl.when(z == 0)
        def _():
            self.add(z, [(self.landed, z), (self.chain, nf)], target)

        @pl.when(z == nf - 1)
        def _():
            self.add(z, [(self.landed, z), (self.chain, z)], target)

        @pl.when((z > 0) & (z < nf - 1))
        def _():
            self.add(z, [(self.landed, z), (self.chain, z), (self.chain, nf)], target)

    def settle(self):
        z, nf = self.z, self.nf
        self.over(z).wait_send()
        for k in range(nf - 1, 0, -1):

            @pl.when(z + k < nf)
            def _():
                self.over(z + k).wait_send()
                self.right(z + k).wait_send()

            @pl.when(z - k >= 0)
            def _():
                self.over(z - k).wait_send()
                self.left(z - k, k == 1).wait_send()


def in_parts(width):
    rows = -(-width // 64) * 32
    return rows, width - rows


def in_view(source, nf):
    rows, second = in_parts(source.shape[-2])

    def view(block, part):
        here = pl.ds(pl.multiple_of(part * second, 16), rows)
        if len(source.shape) == 3:
            return source.at[block, here]
        columns = source.shape[1] // nf
        return source.at[here, pl.ds(pl.multiple_of(block * columns, LANES), columns)]

    return view


def out_view(source, nf):
    rows, columns = source.shape[0] // nf, source.shape[1] // 2

    def view(block, part):
        here = pl.ds(pl.multiple_of(block * rows, 16), rows)
        return source.at[here, pl.ds(pl.multiple_of(part * columns, LANES), columns)]

    return view


def in_part_shape(nf, source):
    columns = source.shape[2] if len(source.shape) == 3 else source.shape[1] // nf
    return in_parts(source.shape[-2])[0], columns


def out_part_shape(nf, source):
    return source.shape[0] // nf, source.shape[1] // 2


def section_sum_scratch(nf, part):
    return [
        pltpu.VMEM((nf,) + part, BF16),
        pltpu.VMEM((nf,) + part, BF16),
        pltpu.VMEM((nf + 1,) + part, BF16),
        pltpu.SemaphoreType.DMA((5, nf + 1)),
        pltpu.VMEM(part, BF16),
    ]


class SectionReturn:

    def __init__(self, piece, place, owner, y, sems):
        self.piece, self.place, self.owner, self.y, self.sems = piece, place, owner, y, sems

    def keep(self):
        return pltpu.make_async_copy(self.piece(self.owner), self.place(self.owner), self.sems.at[2])

    def send(self):
        other = 1 - self.owner
        return remote(
            self.piece(other), self.place(other), self.sems.at[0], self.sems.at[1], {"section": 1 - self.y}
        )

    def begin(self):
        @pl.when(self.y == self.owner)
        def _():
            self.keep().start()

        @pl.when(self.y != self.owner)
        def _():
            self.send().start()

    def finish(self):
        @pl.when(self.y == self.owner)
        def _():
            self.keep().wait()
            self.send().wait_recv()

        @pl.when(self.y != self.owner)
        def _():
            self.send().wait_send()


def end_kernel(
    nf, nd,
    in_ref, in_part1_ref, out_part0_ref, out_part1_ref, small0_ref, small1_ref,
    in_all, out_all, small_all,
    in_own, in_landed, in_chain, in_sems, in_part,
    in_final, out_final, small_slots, small_total, local_sem, swap_sem, back_sem, small_sems, group_send, group_recv,
):
    y, z, d = lax.axis_index("section"), lax.axis_index("fsdp"), lax.axis_index("dp")
    away = z != d
    twin = {"fsdp": d, "dp": z}
    peer = {"section": 1 - y}
    wide = lambda k: {"fsdp": (z + k) % nf}
    greet(
        [(None, peer), (away, twin)]
        + [(None, wide(k)) for k in range(1, nf)]
        + [(None, {"dp": flip(d, bit)}) for bit in bits_of(nd)]
    )
    in_sum = SectionSum(in_view(in_ref, nf), nf, y, z, in_own, in_landed, in_chain, in_sems, in_part)
    width = in_final.shape[0]
    part_rows, second = in_parts(width)
    overlap = part_rows - second
    out_rows, out_columns = out_part0_ref.shape
    in_piece = lambda ref: lambda p: ref if p == 0 else ref.at[pl.ds(overlap, width - part_rows)]
    in_place = lambda p: in_final.at[pl.ds(p * part_rows, width - part_rows if p else part_rows)]
    out_place = lambda p: out_final.at[:, pl.ds(p * out_columns, out_columns)]
    out_returns = [
        SectionReturn(lambda p: out_part0_ref, out_place, 0, y, back_sem.at[0]),
        SectionReturn(lambda p: out_part1_ref, out_place, 1, y, back_sem.at[1]),
    ]
    in_returns = [
        SectionReturn(in_piece(in_part), in_place, 0, y, back_sem.at[2]),
        SectionReturn(in_piece(in_part1_ref), in_place, 1, y, back_sem.at[3]),
    ]
    in_groups = [
        GroupRows(
            lambda device, p=p: in_all.at[device, pl.ds(p * part_rows, width - part_rows if p else part_rows)],
            d, nd, group_send.at[p], group_recv.at[p],
        )
        for p in range(2)
    ]
    out_group = GroupRows(rows_of(out_all, out_rows), d, nd, group_send.at[2], group_recv.at[2])
    small_group = GroupRows(lambda device: small_all.at[device], d, nd, group_send.at[3], group_recv.at[3])

    def small_over(ref):
        return remote(ref, small_slots.at[nf], small_sems.at[0, 0], small_sems.at[1, 0], peer)

    def small_load(ref):
        return pltpu.make_async_copy(ref, small_slots.at[0], local_sem.at[0])

    small_copies = [
        remote(small_slots.at[0], small_slots.at[k], small_sems.at[0, k], small_sems.at[1, k], wide(k))
        for k in range(1, nf)
    ]
    small_own = pltpu.make_async_copy(small_total, small_group.part(0), local_sem.at[0])
    swap_target = out_all.at[pl.ds(pl.multiple_of(z * out_rows, 16), out_rows)]
    swap = remote(out_final, swap_target, swap_sem.at[0], swap_sem.at[1], twin)
    stay = pltpu.make_async_copy(out_final, out_group.part(0), swap_sem.at[2])

    def own_copy(p):
        return pltpu.make_async_copy(in_place(p), in_groups[p].part(0), local_sem.at[1 + p])

    def spread(p):
        own_copy(p).start()
        in_groups[p].begin(in_place(p))

    for back in out_returns:
        back.begin()
    in_sum.begin()
    for section, (mine, other) in enumerate(((small0_ref, small1_ref), (small1_ref, small0_ref))):

        @pl.when(y == section)
        def _():
            small_over(other).start()
            small_load(mine).start()


    @pl.when(y == 1)
    def _():
        in_returns[1].keep().start()
        in_returns[1].keep().wait()
        spread(1)

    for back in out_returns:
        back.finish()

    @pl.when(away)
    def _():
        swap.start()

    @pl.when(jnp.logical_not(away))
    def _():
        stay.start()

    for k in range(nf - 1, 0, -1):
        in_sum.stage(k)
        if k == nf - 1:
            small_load(small0_ref).wait()
            small_over(small0_ref).wait()
            small_slots[0] = small_slots[0] + small_slots[nf]
            for copy in small_copies:
                copy.start()

            @pl.when(away)
            def _():
                swap.wait()

            @pl.when(jnp.logical_not(away))
            def _():
                stay.wait()

            out_group.begin()
        if k == nf - 2:
            for copy in small_copies:
                copy.wait()
            total = small_slots[0]
            for j in range(1, nf):
                total = total + small_slots[j]
            small_total[...] = total
            small_own.start()
            small_group.begin(small_total)
            out_group.relay()
        if k == 1:
            small_group.finish()
            small_own.wait()
            out_group.close()
    in_sum.finish()

    @pl.when(y == 0)
    def _():
        in_returns[0].keep().start()
        in_returns[1].send().start()
        in_returns[0].keep().wait()
        spread(0)
        in_returns[0].send().wait_recv()
        spread(1)
        in_returns[1].send().wait_send()

    @pl.when(y == 1)
    def _():
        in_returns[0].send().start()
        in_returns[1].send().wait_recv()
        spread(0)
        in_returns[0].send().wait_send()

    for p in range(2):
        in_groups[p].finish()
        own_copy(p).wait()
    in_sum.settle()


def run_end(nf, nd, in_grad, in_part1, out_part0, out_part1, small0, small1):
    anywhere = pl.BlockSpec(memory_space=pl.ANY)
    dma = pltpu.SemaphoreType.DMA
    width = in_grad.shape[-2]
    out_rows = out_part0.shape[0]
    return pl.pallas_call(
        functools.partial(end_kernel, nf, nd),
        in_specs=[anywhere] * 6,
        out_specs=[anywhere] * 3,
        out_shape=[
            jax.ShapeDtypeStruct((nd, width, in_part1.shape[1]), BF16),
            jax.ShapeDtypeStruct((nd * out_rows, D), BF16),
            jax.ShapeDtypeStruct((nd,) + small0.shape, F32),
        ],
        scratch_shapes=section_sum_scratch(nf, in_part1.shape)
        + [
            pltpu.VMEM((width, in_part1.shape[1]), BF16),
            pltpu.VMEM((out_rows, D), BF16),
            pltpu.VMEM((nf + 1,) + small0.shape, F32),
            pltpu.VMEM(small0.shape, F32),
            dma((3,)),
            dma((3,)),
            dma((4, 3)),
            dma((2, nf)),
            dma((4, nd)),
            dma((4, nd)),
        ],
        compiler_params=pltpu.CompilerParams(
            vmem_limit_bytes=VMEM_LIMIT, collective_id=6, has_side_effects=True
        ),
        name="sum_end",
    )(in_grad, in_part1, out_part0, out_part1, small0, small1)


def finish_kernel(
    ch, nd, in_ref, shared_ref, out_ref, small_ref,
    in_total, out_total, gain_ref, convw_ref, convb_ref, dtb_ref, alog_ref, skip_ref, gate_ref, shared, sems,
):
    step = pl.program_id(0)
    heads = H // nd
    count = DIN - 2 * DI

    def copy(j):
        return pltpu.make_async_copy(shared_ref.at[j, pl.ds(2 * ch, count)], shared.at[j], sems.at[j])

    @pl.when(step == 0)
    def _():
        for j in range(nd):
            copy(j).start()
        for row, (start, size) in enumerate(gain_rows(small_ref.shape[2])):
            gain_ref[:, start : start + size] = jnp.sum(small_ref[:, 8 + row : 9 + row, 0:size], axis=0)
        both = jnp.sum(small_ref[:, 0:8, ch:], axis=0)
        convw_ref[:, DI:] = both[0:4, :]
        convb_ref[:, DI:] = both[4:5, :]
        rows = lax.broadcasted_iota(jnp.int32, (ch, LANES), 0)
        columns = lax.broadcasted_iota(jnp.int32, (ch, LANES), 1)
        by_head = jnp.where(rows // P_SIZE == columns, 1.0, 0.0)
        decays, skips = [[], []], []
        for j in range(nd):
            here = slice(j * ch, (j + 1) * ch)
            convw_ref[:, here] = small_ref[j, 0:4, :ch]
            convb_ref[:, here] = small_ref[j, 4:5, :ch]
            gate_ref[:, here] = small_ref[j, 5:6, :ch]
            skips.append(fine_dot(small_ref[j, 0:8, :ch], by_head)[6:7, :heads])
            for k in range(2):
                decays[k].append(small_ref[j, 7:8, k * LANES : k * LANES + heads])
        dtb_ref[...] = jnp.concatenate(decays[0], axis=1)
        alog_ref[...] = jnp.concatenate(decays[1], axis=1)
        skip_ref[...] = jnp.concatenate(skips, axis=1)

    @pl.when(step < 2 * nd)
    def _():
        in_total[...] = in_ref[...].astype(F32)
        out_total[...] = out_ref[...].astype(F32)

    @pl.when(step == 2 * nd)
    def _():
        for j in range(nd):
            copy(j).wait()
        total = shared[0].astype(F32)
        for j in range(1, nd):
            total = total + shared[j].astype(F32)
        in_total[0:count, :] = total


def run_finish(ch, nd, in_all, out_all, small_all):
    columns = in_all.shape[2]
    rows = out_all.shape[0]
    piece = rows // (2 * nd)
    final = lambda s: (jnp.minimum(s, 2 * nd - 1), 0)

    def in_block(s):
        s = jnp.minimum(s, 2 * nd - 1)
        return (s % nd, s // nd, 0)

    smalls = [(1, D), (K, DC), (1, DC), (1, H), (1, H), (1, H), (1, DI)]
    return pl.pallas_call(
        functools.partial(finish_kernel, ch, nd),
        grid=(2 * nd + 1,),
        in_specs=[
            pl.BlockSpec((None, ch, columns), in_block),
            pl.BlockSpec(memory_space=pl.ANY),
            pl.BlockSpec((piece, D), final),
            once(small_all.shape),
        ],
        out_specs=[pl.BlockSpec((ch, columns), lambda s: (s, 0)), pl.BlockSpec((piece, D), final)]
        + [once(shape) for shape in smalls],
        out_shape=[jax.ShapeDtypeStruct((DIN, columns), F32), jax.ShapeDtypeStruct((rows, D), F32)]
        + [jax.ShapeDtypeStruct(shape, F32) for shape in smalls],
        scratch_shapes=[pltpu.VMEM((nd, DIN - 2 * DI, columns), BF16), pltpu.SemaphoreType.DMA((nd,))],
        compiler_params=pltpu.CompilerParams(vmem_limit_bytes=VMEM_LIMIT),
        name="finish",
    )(in_all, in_all, out_all, small_all)


class Weights:

    def __init__(self, source, held, sems):
        self.source, self.held, self.sems = source, held, sems
        self.blocks = source.shape[0]
        self.columns = source.shape[2]

    def copies(self):
        out = []
        for k in range(self.blocks):
            if len(self.held.shape) == 3:
                target = self.held.at[k]
            else:
                target = self.held.at[:, pl.ds(k * self.columns, self.columns)]
            out.append(pltpu.make_async_copy(self.source.at[k], target, self.sems.at[k]))
        return out

    def forward(self, rows):
        if len(self.held.shape) == 2:
            return dot(rows, self.held[...], ((1,), (1,)))
        total = 0.0
        for k in range(self.blocks):
            total = total + dot(
                rows[:, k * self.columns : (k + 1) * self.columns], self.held[k], ((1,), (1,))
            )
        return total

    def backward(self, rows):
        if len(self.held.shape) == 2:
            return dot(rows, self.held[...])
        return jnp.concatenate([dot(rows, self.held[k]) for k in range(self.blocks)], axis=1)


def held_shape(w_in):
    blocks, width, columns = w_in.shape
    return (width, blocks * columns) if columns % LANES == 0 else (blocks, width, columns)


def own_steps(steps, turn):
    padded = jnp.concatenate([steps, jnp.zeros((steps.shape[0], LANES - H), F32)], axis=1)
    return pltpu.roll(padded, LANES - turn, 1)


def mix_forward(
    ch, proj_ref, meta_ref, segrow_ref, conv_w_ref, conv_b_ref, dtb_ref, alog_ref, skip_ref,
    gated_ref, square_ref, mixed_ref, pre_ref, state_out_ref, pad, state, sub, turn,
):
    conv_width = ch + 2 * N
    rows = pl.ds(pl.multiple_of(sub * Q, Q), Q)
    meta = meta_ref[rows, :]
    pad[8:, :] = proj_ref[rows, ch : ch + conv_width]
    pre = conv_b_ref[...] + conv_w_ref[3:4, :] * pad[8:, :]
    for lag in range(1, K):
        pre = pre + (conv_w_ref[3 - lag : 4 - lag, :] * meta[:, lag : lag + 1]) * pad[8 - lag : 8 - lag + Q, :]
    pad[0:8, :] = pad[Q : Q + 8, :]
    pre_ref[rows, :] = pre
    conv_out = pre * jax.nn.sigmoid(pre)
    values = conv_out[:, :ch]
    b_part = conv_out[:, ch : ch + N]
    c_part = conv_out[:, ch + N :]
    row, column = triangles()
    tri = jnp.where(row >= column, 1.0, 0.0)
    shifted, step, log_decay, cumulative = decay_tables(
        own_steps(proj_ref[rows, ch + conv_width :], turn), dtb_ref[...], alog_ref[...], tri
    )
    linked = (row >= column) & (meta[:, 0:1] == segrow_ref[sub])
    inner = jnp.where(linked, split_dot(c_part, b_part, ((1,), (1,))), 0.0)
    cum_t = cumulative.T
    step_t = step.T
    last = cumulative[Q - 1 : Q, :]
    entry = meta[:, 4:5] * jnp.exp(cumulative)
    weight = meta[:, 5:6] * jnp.exp(last - cumulative) * step
    state_in = state[...]
    state_out_ref[sub] = state_in
    carried = split_dot(c_part, state_in)
    low_half = lax.broadcasted_iota(jnp.int32, (Q, LANES), 1) < P_SIZE
    squares = jnp.zeros((Q, 1), F32)
    weighted = []
    entries = []
    values_high, values_low = halves(values)
    for pair in range(ch // LANES):
        lanes = slice(pair * LANES, (pair + 1) * LANES)
        values_pair = values[:, lanes]
        mats = []
        for head in (2 * pair, 2 * pair + 1):
            spread = jnp.minimum(cumulative[:, head : head + 1] - cum_t[head : head + 1, :], 0.0)
            mats.append((inner * jnp.exp(spread) * step_t[head : head + 1, :]).astype(BF16))
        parts = [values_high[:, lanes], values_low[:, lanes]]
        zero = jnp.zeros_like(parts[0])
        stacked = jnp.concatenate(
            [
                jnp.concatenate([jnp.where(low_half, part, zero) for part in parts], axis=1),
                jnp.concatenate([jnp.where(low_half, zero, part) for part in parts], axis=1),
            ],
            axis=0,
        )
        both = dot(jnp.concatenate(mats, axis=1), stacked)
        out = both[:, :LANES] + both[:, LANES:]
        entry_pair = pair_lanes(entry, 2 * pair, low_half)
        out = out + entry_pair * carried[:, lanes] + skip_ref[:, lanes] * values_pair
        mixed_ref[rows, lanes] = out
        gate = proj_ref[rows, lanes]
        gated = out * (gate * jax.nn.sigmoid(gate))
        squares = squares + jnp.sum(gated * gated, axis=1, keepdims=True)
        gated_ref[rows, lanes] = gated
        weighted.append(pair_lanes(weight, 2 * pair, low_half) * values_pair)
        entries.append(entry_pair[Q - 1 : Q, :])
    square_ref[0, pl.ds(sub, 1), :] = to_row(squares)
    state[...] = jnp.concatenate(entries, axis=1) * state_in + split_dot(
        b_part.T, jnp.concatenate(weighted, axis=1)
    )


def first_kernel(
    ch, nf, nd,
    x_ref, cot_ref, seg_ref, in_ref, out_ref, conv_w_ref, conv_b_ref, norm_ref, gate_ref, head_ref,
    proj_ref, mixed_ref, pre_ref, state_out_ref, nout_ref, branch_ref, next_ref, ratio_ref,
    conv_w_out, conv_b_out, dtb_out, alog_out, skip_out, gain_out, norm_out, meta_out, segrow_out,
    normed_all, moved_ref, hidden_out, cot_own, w_in0, w_in1, w_out0, w_out1,
    held, w_out, pad, state, gated, partial, landed, squares, low, normed, x_low, table, seg_all, own_block, staged,
    sum_send, sum_recv, tile_send, tile_recv, group_send, group_recv, start_send, start_recv, deal_send, deal_recv,
    in_sems0, in_sems1, out_sems0, out_sems1, local_sem, load_sem, small_sem, swap_sem, own_sem,
):
    step = pl.program_id(0)
    y, z, d = lax.axis_index("section"), lax.axis_index("fsdp"), lax.axis_index("dp")
    block = proj_ref.shape[0]
    subs = block // Q
    rows = block // nd
    length = block * nf
    lines = block // Q * 8
    heads = H // nd
    bits = bits_of(nd)
    twin = {"fsdp": d, "dp": z}
    home = z == d
    away = z != d
    peer = {"section": 1 - y}
    blocks = BlockSum(partial, landed, d, nd, sum_send, sum_recv)
    weights = Weights(w_in0, held, load_sem)
    out_load = pltpu.make_async_copy(w_out0, w_out, local_sem.at[0])
    gathers = [SectionGather(w_in0, 0, nf, y, z, in_sems0, own_block), SectionGather(w_in1, 1, nf, y, z, in_sems1, own_block)]
    outs = [
        OutGather(out_ref, w_out0, 0, nf, y, z, d, out_sems0, staged),
        OutGather(out_ref, w_out1, 1, nf, y, z, d, out_sems1, staged),
    ]
    enter = Deal(x_ref.at[y], x_low, nf, nd, z, d, deal_send.at[0], deal_recv.at[0], False)
    enter_cot = Deal(cot_ref.at[y], cot_own, nf, nd, z, d, deal_send.at[1], deal_recv.at[1], False)
    first_group = GroupRows(lambda device: normed.at[:, device], d, nd, start_send.at[0], start_recv.at[0])
    normed_copy = pltpu.make_async_copy(normed, normed_all, local_sem.at[1])
    hidden_copy = pltpu.make_async_copy(x_low, hidden_out, local_sem.at[2])

    def seg_rows(device):
        return seg_all.at[pl.ds(pl.multiple_of(device * lines, 8), lines)]

    seg_group = GroupRows(seg_rows, d, nd, start_send.at[1], start_recv.at[1])

    def every(place):
        return GroupRows(lambda device: moved_ref.at[place, device], d, nd, group_send.at[place], group_recv.at[place])

    def mine(place):
        return pltpu.make_async_copy(low.at[place], moved_ref.at[place, d], local_sem.at[3 + place])

    def stage(gather, k):
        gather.arrive(k)
        gather.relay(k)

    @pl.when(step == 0)
    def _():
        greet(
            line_neighbours(nf, y, z)
            + [(away, twin)]
            + deal_partners(nf, nd, z, d)
            + [(None, {"dp": flip(d, j)}) for j in range(1, nd)]
        )

        own_copies = [
            pltpu.make_async_copy(
                in_ref.at[pl.ds(pl.multiple_of(begin, 16), count)], own_block.at[pl.ds(spot, count)], own_sem.at[k]
            )
            for k, (begin, spot, count) in enumerate(
                [(d * ch, 0, ch), (DI + d * ch, ch, ch), (2 * DI, 2 * ch, DIN - 2 * DI)]
            )
        ]
        for copy in own_copies:
            copy.start()
        for copy in own_copies:
            copy.wait()
        gathers[0].start_cross()
        gathers[1].start_cross()
        table[y, 0:4, :] = conv_w_ref[...]
        table[y, 4:5, :] = conv_b_ref[...]
        table[y, 5:6, 0:D] = norm_ref[...]
        table[y, 6:7, 0:DI] = gate_ref[...]
        for k in range(3):
            table[y, 7:8, k * LANES : (k + 1) * LANES] = head_ref[k : k + 1, :]
        small_copy = remote(table.at[y], table.at[y], small_sem.at[0], small_sem.at[1], peer)
        small_copy.start()
        seg_swap = remote(seg_ref, seg_rows(z), swap_sem.at[0], swap_sem.at[1], twin)
        seg_stay = pltpu.make_async_copy(seg_ref, seg_rows(d), swap_sem.at[0])

        @pl.when(away)
        def _():
            seg_swap.start()

        @pl.when(home)
        def _():
            seg_stay.start()

        gathers[0].begin()
        enter.start_all()
        outs[0].begin()
        stage(gathers[0], 1)
        outs[0].begin_other()
        outs[0].hops(1)

        small_copy.wait()
        enter.arrive()
        hidden_copy.start()
        values = x_low[...].astype(F32)
        low[...] = (values * rms_parts(values) * table[0, 5:6, 0:D]).astype(BF16)
        for place in range(nf):
            normed[place, d] = low[place]
        first_group.begin(low)

        @pl.when(away)
        def _():
            seg_swap.wait()

        @pl.when(home)
        def _():
            seg_stay.wait()

        seg_group.begin()
        for k in range(2, nf - 1):
            stage(gathers[0], k)
            outs[0].hops(k)

        turn = d * heads
        low_half = lax.broadcasted_iota(jnp.int32, (1, LANES), 1) < P_SIZE
        channels = pl.ds(pl.multiple_of(d * ch, LANES), ch)
        for section in range(2):
            conv_w_out[section, :, 0:ch] = table[section, 0:4, channels]
            conv_w_out[section, :, ch:] = table[section, 0:4, DI:DC]
            conv_b_out[section, :, 0:ch] = table[section, 4:5, channels]
            conv_b_out[section, :, ch:] = table[section, 4:5, DI:DC]
            norm_out[section] = table[section, 5:6, 0:D]
            gain_out[section] = table[section, 6:7, channels]
            head_rows = [
                pltpu.roll(table[section, :, k * LANES : (k + 1) * LANES], LANES - turn, 1)[7:8, :] for k in range(3)
            ]
            dtb_out[section] = head_rows[0]
            alog_out[section] = head_rows[1]
            for pair in range(ch // LANES):
                skip_out[section, :, pair * LANES : (pair + 1) * LANES] = pair_lanes(head_rows[2], 2 * pair, low_half)

        seg_group.finish()

        lane = lax.broadcasted_iota(jnp.int32, (8, LANES), 1)
        sub_lane = lax.broadcasted_iota(jnp.int32, (Q, LANES), 1)
        before = jnp.full((8, LANES), -1.0, F32)
        for chunk in range(length // Q):
            now = seg_all[chunk * 8 : chunk * 8 + 8, :]
            segrow_out[chunk] = now[0:1, :]
            columns = [now[0:1, :]]
            for lag in range(1, K):
                earlier = jnp.where(lane < lag, pltpu.roll(before, lag, 1), pltpu.roll(now, lag, 1))
                columns.append(jnp.where(earlier == now, 1.0, 0.0)[0:1, :])
            columns.append(jnp.where(now == before[:, Q - 1 : Q], 1.0, 0.0)[0:1, :])
            columns.append(jnp.where(now == now[:, Q - 1 : Q], 1.0, 0.0)[0:1, :])
            masks = jnp.zeros((Q, LANES), F32)
            for j, row in enumerate(columns):
                masks = jnp.where(sub_lane == j, to_column(row), masks)
            meta_out[chunk * Q : (chunk + 1) * Q, :] = masks
            before = now

        stage(gathers[0], nf - 1)
        outs[0].hops(nf - 1)
        outs[0].hand_over()
        gathers[1].begin()
        first_group.finish()
        normed_copy.start()
        pad[0:8, :] = jnp.zeros((8, pad.shape[1]), F32)
        state[...] = jnp.zeros_like(state)
        for k in range(1, nf):
            gathers[0].settle(k)
        gathers[0].settle_begin()
        for copy in weights.copies():
            copy.start()
        for copy in weights.copies():
            copy.wait()

    def tile(place):
        return GroupTiles(squares.at[place], tile_send.at[place], tile_recv.at[place], d, nd)

    def project(place):
        ratio = lax.rsqrt(tile(place).finish() * (1.0 / DI) + EPSILON)
        for sub in range(subs):
            piece = place * subs + sub
            ratio_ref[pl.ds(piece, 1), :] = ratio[sub : sub + 1, :]
            normed_out = gated[place % 2, sub * Q : (sub + 1) * Q, :] * to_column(ratio[sub : sub + 1, :])
            nout_ref[pl.ds(pl.multiple_of(piece * Q, Q), Q), :] = (normed_out * gain_out[0]).astype(BF16)
        here_rows = pl.ds(pl.multiple_of(place * block, Q), block)
        product = dot(nout_ref[here_rows, :], w_out[...])
        for o in range(nd):
            partial[place, o] = product[o * rows : (o + 1) * rows, :]
        blocks.send(0, place)

    def pass_on(place):
        for k in range(1, len(bits)):
            blocks.send(k, place)

    def conclude(place):
        branch = blocks.own(place)
        branch_ref[place] = branch
        moved = (x_low[place].astype(F32) + branch).astype(BF16)
        next_ref[place] = moved
        values = moved.astype(F32)
        low[place] = (values * rms_parts(values) * norm_out[1]).astype(BF16)
        mine(place).start()
        every(place).begin(low.at[place])

    proj_ref[...] = weights.forward(normed[step].reshape(block, D))

    @pl.when(step == 0)
    def _():
        stage(gathers[1], 1)

    @pl.when(step == 1)
    def _():
        outs[0].settle()
        out_load.start()
        out_load.wait()

    @pl.when(step >= 1)
    def _():
        project(step - 1)

    meta = meta_out.at[pl.ds(pl.multiple_of(step * block, Q), block)]
    segrow = segrow_out.at[pl.ds(step * subs, subs)]

    def one_chunk(sub, carry):
        mix_forward(
            ch, proj_ref, meta, segrow, conv_w_out.at[0], conv_b_out.at[0], dtb_out.at[0], alog_out.at[0],
            skip_out.at[0], gated.at[step % 2], squares.at[step], mixed_ref, pre_ref, state_out_ref, pad, state, sub,
            d * heads,
        )

        @pl.when(sub == 0)
        def _():
            @pl.when(step >= 2)
            def _():
                conclude(step - 2)

            @pl.when(step >= 1)
            def _():
                pass_on(step - 1)

            @pl.when(step >= 3)
            def _():
                every(step - 3).relay()

            for k in range(2, nf):

                @pl.when(step == k - 1)
                def _():
                    stage(gathers[1], k)


        return carry

    lax.fori_loop(0, subs, one_chunk, 0)
    tile(step).begin()

    @pl.when(step == 1)
    def _():
        outs[1].begin()

    @pl.when(step == nf - 2)
    def _():
        enter_cot.start_all()

    @pl.when(step == 2)
    def _():
        outs[1].begin_other()

    for k in range(1, nf):

        @pl.when(step == min(k + 1, nf - 1))
        def _():
            outs[1].hops(k)
            if k == nf - 1:
                outs[1].hand_over()

    @pl.when(step == nf - 1)
    def _():
        project(nf - 1)
        pass_on(nf - 1)
        conclude(nf - 2)
        every(nf - 3).relay()
        conclude(nf - 1)
        every(nf - 2).relay()
        for k in range(1, nf):
            gathers[1].settle(k)
        gathers[1].settle_begin()
        outs[1].settle()
        enter.settle()
        enter_cot.arrive()
        enter_cot.settle()
        normed_copy.wait()
        hidden_copy.wait()
        every(nf - 1).relay()
        for place in range(nf):
            every(place).close()
            mine(place).wait()
        blocks.settle(nf)


def run_first(ch, nf, nd, x, cot, seg, in_rows, out_rows, conv_w, conv_b, norm_gain, gate_gain, head_table, identity):
    block = x.shape[1]
    length = block * nf
    conv_width = ch + 2 * N
    columns = in_rows.shape[1]
    width = 2 * ch + DIN - 2 * DI
    pieces = length // Q
    subs = block // Q
    bits = len(bits_of(nd))
    own = (nf, block // nd, D)
    every = (nf, nd, block // nd, D)
    w_in = jax.ShapeDtypeStruct((nf, width, columns), BF16)
    anywhere = pl.BlockSpec(memory_space=pl.ANY)
    dma = pltpu.SemaphoreType.DMA
    ordered = lambda s: (s, 0)
    small = [(2, K, conv_width), (2, 1, conv_width), (2, 1, LANES), (2, 1, LANES), (2, 1, ch), (2, 1, ch), (2, 1, D)]
    resident = small + [(length, LANES), (pieces, 1, Q)]
    return pl.pallas_call(
        functools.partial(first_kernel, ch, nf, nd),
        grid=(nf,),
        in_specs=[anywhere] * 5 + [once(part.shape) for part in (conv_w, conv_b, norm_gain, gate_gain, head_table)],
        out_specs=[
            pl.BlockSpec((block, width), ordered),
            pl.BlockSpec((block, ch), ordered),
            pl.BlockSpec((block, conv_width), ordered),
            pl.BlockSpec((subs, N, ch), lambda s: (s, 0, 0)),
            once((length, ch)),
            once(own),
            once(own),
            once((pieces, Q)),
        ]
        + [once(shape) for shape in resident]
        + [anywhere] * 8,
        out_shape=[
            jax.ShapeDtypeStruct((length, width), F32),
            jax.ShapeDtypeStruct((length, ch), F32),
            jax.ShapeDtypeStruct((length, conv_width), F32),
            jax.ShapeDtypeStruct((pieces, N, ch), F32),
            jax.ShapeDtypeStruct((length, ch), BF16),
            jax.ShapeDtypeStruct(own, F32),
            jax.ShapeDtypeStruct(own, BF16),
            jax.ShapeDtypeStruct((pieces, Q), F32),
        ]
        + [jax.ShapeDtypeStruct(shape, F32) for shape in resident]
        + [
            jax.ShapeDtypeStruct(every, BF16),
            jax.ShapeDtypeStruct(every, BF16),
            jax.ShapeDtypeStruct(own, BF16),
            jax.ShapeDtypeStruct(own, BF16),
            w_in,
            w_in,
            jax.ShapeDtypeStruct((ch, D), BF16),
            jax.ShapeDtypeStruct((ch, D), BF16),
        ],
        scratch_shapes=[
            pltpu.VMEM(held_shape(w_in), BF16),
            pltpu.VMEM((ch, D), BF16),
            pltpu.VMEM((Q + 8, conv_width), F32),
            pltpu.VMEM((N, ch), F32),
            pltpu.VMEM((2, block, ch), F32),
            pltpu.VMEM(every, F32),
            pltpu.VMEM((bits, nf, nd // 2, block // nd, D), F32),
            pltpu.VMEM((nf, nd, 8, LANES), F32),
            pltpu.VMEM(own, BF16),
            pltpu.VMEM(every, BF16),
            pltpu.VMEM(own, BF16),
            pltpu.VMEM((2, 8, DC), F32),
            pltpu.VMEM((pieces * 8, LANES), F32),
            pltpu.VMEM((width, columns), BF16),
            pltpu.VMEM((ch, D), BF16),
            dma((bits, nf, nd)),
            dma((bits, nf, nd)),
            dma((nf, nd)),
            dma((nf, nd)),
            dma((nf, nd)),
            dma((nf, nd)),
            dma((2, nd)),
            dma((2, nd)),
            dma((2, nf)),
            dma((2, nf)),
            dma((7, 2 * nf)),
            dma((7, 2 * nf)),
            dma((6, 4)),
            dma((6, 4)),
            dma((3 + nf,)),
            dma((nf,)),
            dma((2,)),
            dma((2,)),
            dma((3,)),
        ],
        compiler_params=pltpu.CompilerParams(
            vmem_limit_bytes=VMEM_LIMIT, collective_id=identity, has_side_effects=True
        ),
        name="layer_first",
    )(x, cot, seg, in_rows, out_rows, conv_w, conv_b, norm_gain, gate_gain, head_table)


def layer_kernel(
    ch, nf, nd,
    normed_ref, meta_ref, segrow_ref, conv_w_ref, conv_b_ref, dtb_ref, alog_ref, skip_ref, gain_ref,
    w_in_ref, w_out_ref, hidden_ref, extra_ref,
    proj_ref, nout_ref, mixed_ref, pre_ref, state_out_ref, branch_ref, next_ref, ratio_ref, pull_ref, cot_all,
    held, w_out, pad, state, gated, partial, landed, squares, pulls,
    sum_send, sum_recv, tile_send, tile_recv, group_send, group_recv, local_sem, load_sem,
):
    step = pl.program_id(0)
    y, z, d = lax.axis_index("section"), lax.axis_index("fsdp"), lax.axis_index("dp")
    block = normed_ref.shape[0]
    subs = block // Q
    rows = block // nd
    bits = bits_of(nd)
    blocks = BlockSum(partial, landed, d, nd, sum_send, sum_recv)
    weights = Weights(w_in_ref, held, load_sem)
    out_load = pltpu.make_async_copy(w_out_ref, w_out, local_sem.at[0])
    cot_group = GroupRows(lambda device: cot_all.at[:, device], d, nd, group_send.at[0], group_recv.at[0])
    cot_keep = pltpu.make_async_copy(extra_ref, cot_group.part(0), local_sem.at[1])

    @pl.when(step == 0)
    def _():
        for copy in weights.copies():
            copy.start()
        out_load.start()
        greet([(None, {"dp": flip(d, j)}) for j in range(1, nd)])
        cot_keep.start()
        cot_group.begin(extra_ref)
        pad[0:8, :] = jnp.zeros((8, pad.shape[1]), F32)
        state[...] = jnp.zeros_like(state)
        pulls[0] = jnp.zeros(pulls.shape[1:], F32)
        for copy in weights.copies():
            copy.wait()
        out_load.wait()

    def tile(place):
        return GroupTiles(squares.at[place], tile_send.at[place], tile_recv.at[place], d, nd)

    def project(place):
        ratio = lax.rsqrt(tile(place).finish() * (1.0 / DI) + EPSILON)
        for sub in range(subs):
            piece = place * subs + sub
            ratio_ref[pl.ds(piece, 1), :] = ratio[sub : sub + 1, :]
            normed_out = gated[place % 2, sub * Q : (sub + 1) * Q, :] * to_column(ratio[sub : sub + 1, :])
            nout_ref[pl.ds(pl.multiple_of(piece * Q, Q), Q), :] = (normed_out * gain_ref[...]).astype(BF16)
        here_rows = pl.ds(pl.multiple_of(place * block, Q), block)
        product = dot(nout_ref[here_rows, :], w_out[...]).astype(partial.dtype)
        for o in range(nd):
            partial[place, o] = product[o * rows : (o + 1) * rows, :]
        blocks.send(0, place)

    def pass_on(place):
        for k in range(1, len(bits)):
            blocks.send(k, place)

    def conclude(place):
        branch = blocks.own(place)
        branch_ref[place] = branch
        moved = (hidden_ref[place].astype(F32) + branch).astype(BF16)
        next_ref[place] = moved
        first = place * block + d * rows
        pulls[0, pl.ds(first // Q, 1), :] += to_row(
            jnp.sum(extra_ref[place].astype(F32) * branch, axis=1, keepdims=True), first % Q
        )

    proj_ref[...] = weights.forward(normed_ref[...])

    @pl.when(step >= 1)
    def _():
        project(step - 1)

    def one_chunk(sub, carry):
        mix_forward(
            ch, proj_ref, meta_ref, segrow_ref, conv_w_ref, conv_b_ref, dtb_ref, alog_ref, skip_ref,
            gated.at[step % 2], squares.at[step], mixed_ref, pre_ref, state_out_ref, pad, state, sub, d * (H // nd),
        )

        @pl.when(sub == 0)
        def _():
            @pl.when(step >= 2)
            def _():
                conclude(step - 2)

            @pl.when(step >= 1)
            def _():
                pass_on(step - 1)

        return carry

    lax.fori_loop(0, subs, one_chunk, 0)
    tile(step).begin()

    @pl.when(step == min(2, nf - 1))
    def _():
        cot_group.relay()

    @pl.when(step == nf - 1)
    def _():
        project(nf - 1)
        pass_on(nf - 1)
        conclude(nf - 2)
        conclude(nf - 1)
        pull_ref[...] = group_tiles(pulls, group_send.at[1], group_recv.at[1], d, nd)
        cot_group.close()
        cot_keep.wait()
        blocks.settle(nf)


def once(shape):
    return pl.BlockSpec(shape, lambda s: (0,) * len(shape), pipeline_mode=pl.Buffered(buffer_count=1))


def pick(part, layer):
    return pl.BlockSpec(
        (None,) + part.shape[1:], lambda s: (layer, 0, 0), pipeline_mode=pl.Buffered(buffer_count=1)
    )


def run_layer(
    ch, rows, nf, nd, normed_all, meta, segrow, small, w_in, w_out, hidden, extra, identity
):
    length, width = normed_all.shape[0], w_in.shape[1]
    layer = 1
    conv_width = ch + 2 * N
    block = rows
    steps = nf
    pieces = length // Q
    subs = block // Q
    own = (nf, rows // nd, D)
    every = (nf, nd, rows // nd, D)
    bits = len(bits_of(nd))
    dma = pltpu.SemaphoreType.DMA
    anywhere = pl.BlockSpec(memory_space=pl.ANY)
    ordered = lambda s: (s, 0)
    ordered3 = lambda s: (s, 0, 0)
    return pl.pallas_call(
        functools.partial(layer_kernel, ch, nf, nd),
        grid=(steps,),
        in_specs=[
            pl.BlockSpec((block, D), ordered),
            pl.BlockSpec((block, LANES), ordered),
            pl.BlockSpec((subs, 1, Q), ordered3),
        ]
        + [pick(part, layer) for part in small]
        + [
            anywhere,
            anywhere,
            once(own),
            once(own),
        ],
        out_specs=[
            pl.BlockSpec((block, width), ordered),
            once((length, ch)),
            pl.BlockSpec((block, ch), ordered),
            pl.BlockSpec((block, conv_width), ordered),
            pl.BlockSpec((subs, N, ch), ordered3),
            once(own),
            once(own),
            once((pieces, Q)),
            once((pieces, Q)),
            anywhere,
        ],
        out_shape=[
            jax.ShapeDtypeStruct((length, width), F32),
            jax.ShapeDtypeStruct((length, ch), BF16),
            jax.ShapeDtypeStruct((length, ch), F32),
            jax.ShapeDtypeStruct((length, conv_width), F32),
            jax.ShapeDtypeStruct((pieces, N, ch), F32),
            jax.ShapeDtypeStruct(own, F32),
            jax.ShapeDtypeStruct(own, BF16),
            jax.ShapeDtypeStruct((pieces, Q), F32),
            jax.ShapeDtypeStruct((pieces, Q), F32),
            jax.ShapeDtypeStruct(every, BF16),
        ],
        scratch_shapes=[
            pltpu.VMEM(held_shape(w_in), BF16),
            pltpu.VMEM((ch, D), BF16),
            pltpu.VMEM((Q + 8, conv_width), F32),
            pltpu.VMEM((N, ch), F32),
            pltpu.VMEM((2, block, ch), F32),
            pltpu.VMEM(every, BF16),
            pltpu.VMEM((bits, nf, nd // 2, rows // nd, D), BF16),
            pltpu.VMEM((steps, nd, 8, LANES), F32),
            pltpu.VMEM((nd, pieces, Q), F32),
            dma((bits, nf, nd)),
            dma((bits, nf, nd)),
            dma((steps, nd)),
            dma((steps, nd)),
            dma((nf, nd)),
            dma((nf, nd)),
            dma((2,)),
            dma((nf,)),
        ],
        compiler_params=pltpu.CompilerParams(
            vmem_limit_bytes=VMEM_LIMIT, collective_id=identity, has_side_effects=True
        ),
        name="layer_last",
    )(normed_all, meta, segrow, *small, w_in, w_out, hidden, extra)


def mix_backward(
    ch, proj_ref, pre_ref, mixed_ref, state_ref, grad_ref, ratio_ref, pull_ref, meta_ref, segrow_ref,
    conv_w_ref, dtb_ref, alog_ref, skip_ref, gain_ref,
    dproj_ref, small_ref, tail, dstate, sub, chunk, turn,
):
    conv_width = ch + 2 * N
    rows = pl.ds(pl.multiple_of(sub * Q, Q), Q)
    meta = meta_ref[rows, :]
    pre = pre_ref[rows, :]
    sig = jax.nn.sigmoid(pre)
    conv_out = pre * sig
    values = conv_out[:, :ch]
    b_part = conv_out[:, ch : ch + N]
    c_part = conv_out[:, ch + N :]
    row, column = triangles()
    tri = jnp.where(row >= column, 1.0, 0.0)
    shifted, step, log_decay, cumulative = decay_tables(
        own_steps(proj_ref[rows, ch + conv_width :], turn), dtb_ref[...], alog_ref[...], tri
    )
    linked = (row <= column) & (meta[:, 0:1] == segrow_ref[sub])
    b_low = b_part.astype(BF16)
    c_low = c_part.astype(BF16)
    inner = jnp.where(linked, dot(b_low, c_low, ((1,), (1,))), 0.0)
    cum_t = cumulative.T
    last = cumulative[Q - 1 : Q, :]
    entry = meta[:, 4:5] * jnp.exp(cumulative)
    weight = meta[:, 5:6] * jnp.exp(last - cumulative)
    state_in = state_ref[sub]
    dstate_in = dstate[...]
    state_low = state_in.astype(BF16)
    dstate_low = dstate_in.astype(BF16)
    carried = dot(c_low, state_low)
    carried_back = dot(b_low, dstate_low)
    low_half = lax.broadcasted_iota(jnp.int32, (Q, LANES), 1) < P_SIZE
    lane = lax.broadcasted_iota(jnp.int32, (Q, LANES), 1)
    ratio = to_column(ratio_ref[pl.ds(chunk, 1), :])
    pull = ratio * ratio * to_column(pull_ref[pl.ds(chunk, 1), :]) * (1.0 / DI)
    dinner = jnp.zeros((Q, Q), F32)
    turned_parts = []
    step_parts, exit_parts, entry_parts = [], [], []
    weighted = []
    entered = []
    entry_rows = []
    dpre_parts = []
    for pair in range(ch // LANES):
        lanes = slice(pair * LANES, (pair + 1) * LANES)
        values_pair = values[:, lanes]
        gate = proj_ref[rows, lanes]
        mixed = mixed_ref[rows, lanes]
        gate_sig = jax.nn.sigmoid(gate)
        gate_silu = gate * gate_sig
        gated = mixed * gate_silu
        scaled = grad_ref[rows, lanes] * ratio
        small_ref[5:6, lanes] += jnp.sum(scaled * gated, axis=0, keepdims=True)
        dgated = scaled * gain_ref[:, lanes] - gated * pull
        dproj_ref[rows, lanes] = (dgated * mixed * (gate_sig + gate_silu * (1.0 - gate_sig))).astype(BF16)
        dmixed = dgated * gate_silu
        small_ref[6:7, lanes] += jnp.sum(dmixed * values_pair, axis=0, keepdims=True)
        zero = jnp.zeros_like(values_pair)
        dmixed_halves = [jnp.where(low_half, dmixed, zero).astype(BF16), jnp.where(low_half, zero, dmixed).astype(BF16)]
        values_low = values_pair.astype(BF16)
        step_pair = pair_lanes(step, 2 * pair, low_half)
        mats = []
        for half, head in enumerate((2 * pair, 2 * pair + 1)):
            spread = jnp.minimum(cum_t[head : head + 1, :] - cumulative[:, head : head + 1], 0.0)
            plain = jnp.exp(spread)
            decay = plain * step[:, head : head + 1]
            product = dot(values_low, dmixed_halves[half], ((1,), (1,)))
            mats.append((inner * plain).astype(BF16))
            spreaded = product * decay
            dinner = dinner + spreaded
            turned_parts.append((spreaded * inner).astype(BF16))
        back = dot(jnp.concatenate(mats, axis=1), jnp.concatenate(dmixed_halves, axis=0))
        weight_pair = pair_lanes(weight, 2 * pair, low_half)
        through = weight_pair * carried_back[:, lanes]
        total = back + through
        dvalues = step_pair * total + skip_ref[:, lanes] * dmixed
        step_parts.append((total * values_pair).astype(BF16))
        exit_parts.append((through * values_pair * step_pair).astype(BF16))
        entry_pair = pair_lanes(entry, 2 * pair, low_half)
        entry_grad = entry_pair * dmixed
        entry_parts.append((entry_grad * carried[:, lanes]).astype(BF16))
        weighted.append((weight_pair * step_pair * values_pair).astype(BF16))
        entered.append(entry_grad.astype(BF16))
        entry_rows.append(entry_pair[Q - 1 : Q, :])
        dpre_parts.append(dvalues)
    weighted = jnp.concatenate(weighted, axis=1)
    entered = jnp.concatenate(entered, axis=1)
    entry_rows = jnp.concatenate(entry_rows, axis=1)
    dinner_low = jnp.where(linked, dinner, 0.0).astype(BF16)
    db = dot(dinner_low, c_low) + dot(weighted, dstate_low, ((1,), (1,)))
    dc = dot(dinner_low.T, b_low) + dot(entered, state_low, ((1,), (1,)))
    state_terms = jnp.sum(state_in * dstate_in, axis=0, keepdims=True) * entry_rows
    head_lane = lax.broadcasted_iota(jnp.int32, (1, LANES), 1)
    state_sum = jnp.zeros((1, LANES), F32)
    for head in range(ch // P_SIZE):
        part = jnp.sum(state_terms[:, head * P_SIZE : (head + 1) * P_SIZE], axis=1, keepdims=True)
        state_sum = state_sum + jnp.where(head_lane == head, part, 0.0)
    heads = ch // P_SIZE

    def marks(shape, place, index):
        return jnp.where(place(shape) == index(shape), 1.0, 0.0).astype(BF16)

    rows_of_shape = lambda shape: lax.broadcasted_iota(jnp.int32, shape, 0)
    columns_of_shape = lambda shape: lax.broadcasted_iota(jnp.int32, shape, 1)
    by_head = marks((ch, LANES), lambda shape: rows_of_shape(shape) // P_SIZE, columns_of_shape)
    dstep = dot(jnp.concatenate(step_parts, axis=1), by_head)
    dexit = dot(jnp.concatenate(exit_parts, axis=1), by_head)
    dcum = dot(jnp.concatenate(entry_parts, axis=1), by_head)
    by_target = marks((LANES, heads * Q), rows_of_shape, lambda shape: columns_of_shape(shape) // Q)
    by_source = marks((heads * Q, LANES), lambda shape: rows_of_shape(shape) // Q, columns_of_shape)
    dcum = dcum + dot(by_target, jnp.concatenate(turned_parts, axis=0)).T
    dcum = dcum - dot(jnp.concatenate(turned_parts, axis=1), by_source)
    later = jnp.where(row <= column, 1.0, 0.0)
    before = jnp.where(row > column, 1.0, 0.0)
    dlog = fine_dot(later, dcum) + fine_dot(before, dexit) + state_sum
    growth = jnp.exp(alog_ref[...])
    dstep = dstep - dlog * growth
    ddt = dstep * jax.nn.sigmoid(shifted)
    small_ref[7:8, 0:LANES] += jnp.sum(ddt, axis=0, keepdims=True)
    small_ref[7:8, LANES : 2 * LANES] += jnp.sum(dlog * log_decay, axis=0, keepdims=True)
    dproj_ref[rows, ch + conv_width :] = pltpu.roll(jnp.where(lane < heads, ddt, 0.0), turn, 1)[:, :H].astype(BF16)
    dstate[...] = entry_rows * dstate_in + dot(c_part.T.astype(BF16), entered)
    dconv_out = jnp.concatenate(dpre_parts + [db, dc], axis=1)
    dpre = dconv_out * (sig + conv_out * (1.0 - sig))
    raw = proj_ref[rows, ch : ch + conv_width]
    small_ref[4:5, :] += jnp.sum(dpre, axis=0, keepdims=True)
    draw = conv_w_ref[3:4, :] * dpre
    small_ref[3:4, :] += jnp.sum(raw * dpre, axis=0, keepdims=True)
    for lag in range(1, K):
        kept = meta[:, lag : lag + 1] * dpre
        tail[lag - 1, 0:Q, :] = kept
        moved = tail[lag - 1, lag : lag + Q, :]
        tail[lag - 1, Q : Q + 8, :] = kept[0:8, :]
        draw = draw + conv_w_ref[3 - lag : 4 - lag, :] * moved
        small_ref[3 - lag : 4 - lag, :] += jnp.sum(raw * moved, axis=0, keepdims=True)
    dproj_ref[rows, ch : ch + conv_width] = draw.astype(BF16)


def gain_rows(width):
    return [(start, min(width, D - start)) for start in range(0, D, width)]


def layer_back_kernel(
    ch, nf, nd, last,
    grad_all_ref, proj_ref, pre_ref, mixed_ref, state_ref, meta_ref, segrow_ref, ratio_ref, pull_ref,
    conv_w_ref, dtb_ref, alog_ref, skip_ref, gain_ref, w_in_ref, w_out_ref,
    hidden_ref, grad_own_ref, norm_gain_ref, branch_ref, *refs,
):
    count = 2 if last else 1
    sources, refs = refs[:count], refs[count:]
    if not last:
        rows_out, refs = refs[0], refs[1:]
    (
        dproj_ref, small_ref, next_ref, next_pull_ref, moved_ref,
    ) = refs[:5]
    results, refs = refs[5 : 5 + count], refs[5 + count :]
    if not last:
        final_ref, refs = refs[0], refs[1:]
    (
        held, w_out, tail, dstate, dnout, partial, landed, pulls, low, dgain,
        sum_send, sum_recv, tile_send, tile_recv, group_send, group_recv, local_sem, load_sem, deal_send, deal_recv,
    ) = refs[:20]
    refs = refs[20:]
    step = pl.program_id(0)
    y, z, d = lax.axis_index("section"), lax.axis_index("fsdp"), lax.axis_index("dp")
    block = grad_all_ref.shape[0]
    subs = block // Q
    rows = block // nd
    bits = bits_of(nd)
    place = nf - 1 - step
    blocks = BlockSum(partial, landed, d, nd, sum_send, sum_recv)
    sums = [
        SectionSum(make(source, nf), nf, y, z, *refs[5 * k : 5 * k + 5])
        for k, (make, source) in enumerate(zip((out_view, in_view), sources))
    ]
    weights = Weights(w_in_ref, held, load_sem)
    out_load = pltpu.make_async_copy(w_out_ref, w_out, local_sem.at[0])
    if last:
        leave = Deal(moved_ref, low, nf, nd, z, d, deal_send, deal_recv, True)
    else:
        leave = Deal(final_ref, rows_out, nf, nd, z, d, deal_send, deal_recv, True)

    def every(place):
        return GroupRows(lambda device: moved_ref.at[place, device], d, nd, group_send.at[place], group_recv.at[place])

    def mine(place):
        return pltpu.make_async_copy(low.at[place], moved_ref.at[place, d], local_sem.at[2 + place])

    @pl.when(step == 0)
    def _():
        for copy in weights.copies():
            copy.start()
        out_load.start()
        greet(
            [(None, {"dp": flip(d, j)}) for j in range(1, nd)]
            + line_neighbours(nf, y, z)
            + deal_partners(nf, nd, z, d)
        )
        for one in sums:
            one.begin()
        if not last:
            leave.start_all()
        tail[...] = jnp.zeros_like(tail)
        dstate[...] = jnp.zeros_like(dstate)
        small_ref[...] = jnp.zeros_like(small_ref)
        dgain[...] = jnp.zeros_like(dgain)
        pulls[0] = jnp.zeros(pulls.shape[1:], F32)
        for copy in weights.copies():
            copy.wait()
        out_load.wait()

    def pass_on(place):
        for k in range(1, len(bits)):
            blocks.send(k, place)

    def conclude(place):
        dnormed = blocks.own(place)
        hidden = hidden_ref[place].astype(F32)
        inverse = rms_parts(hidden)
        dgain[...] += jnp.sum(dnormed * hidden * inverse, axis=0, keepdims=True)
        scaled = dnormed * norm_gain_ref[...]
        dhidden = inverse * (
            scaled - hidden * (inverse * inverse) * jnp.mean(scaled * hidden, axis=1, keepdims=True)
        )
        moved = (grad_own_ref[place].astype(F32) + dhidden).astype(BF16)
        low[place] = moved
        next_ref[place] = moved
        if last:
            leave.start(place)
        else:
            first = place * block + d * rows
            pulls[0, pl.ds(first // Q, 1), :] += to_row(
                jnp.sum(moved.astype(F32) * branch_ref[place], axis=1, keepdims=True), first % Q
            )
            mine(place).start()
            every(place).begin(low.at[place])

    dnout[...] = dot(grad_all_ref[...], w_out[...], ((1,), (1,)))

    @pl.when(step >= 1)
    def _():
        pass_on(place + 1)

    def one_chunk(turn, carry):
        sub = subs - 1 - turn
        mix_backward(
            ch, proj_ref, pre_ref, mixed_ref, state_ref, dnout, ratio_ref, pull_ref, meta_ref, segrow_ref,
            conv_w_ref, dtb_ref, alog_ref, skip_ref, gain_ref,
            dproj_ref, small_ref, tail, dstate, sub, place * subs + sub, d * (H // nd),
        )

        @pl.when((turn == 0) & (step >= 1))
        def _():
            conclude(place + 1)

        return carry

    lax.fori_loop(0, subs, one_chunk, 0)
    product = weights.backward(dproj_ref[...]).astype(BF16)
    for o in range(nd):
        partial[place, o] = product[o * rows : (o + 1) * rows, :]
    blocks.send(0, place)
    if not last:

        @pl.when(step >= 1)
        def _():
            every(place + 1).relay()

    for k in range(nf - 1, 0, -1):

        @pl.when(step == nf - 1 - k)
        def _():
            for one in sums:
                one.stage(k)

    @pl.when(step == nf - 1)
    def _():
        pass_on(0)
        conclude(0)
        for row, (start, size) in enumerate(gain_rows(small_ref.shape[1])):
            small_ref[8 + row : 9 + row, 0:size] = dgain[:, start : start + size]
        if last:
            next_pull_ref[...] = jnp.zeros_like(next_pull_ref)
        else:
            next_pull_ref[...] = group_tiles(pulls, tile_send, tile_recv, d, nd)
        for one, result in zip(sums, results):
            one.finish()
            copy = pltpu.make_async_copy(one.result, result, local_sem.at[1])
            copy.start()
            copy.wait()
            one.settle()
        leave.arrive()
        leave.settle()
        if not last:
            every(0).relay()
            for k in range(nf):
                every(k).close()
                mine(k).wait()
        blocks.settle(nf)


def run_layer_back(
    ch, rows, nf, nd, last, grad_all, proj, pre, mixed, states, meta, segrow, ratio, pull, small, w_in, w_out,
    hidden, grad_own, norm_gain, branch, identity, sums, *leaving,
):
    length, width = proj.shape
    shapes = [make(nf, g) for make, g in zip((out_part_shape, in_part_shape), sums)]
    conv_width = ch + 2 * N
    block = rows
    steps = nf
    own = (nf, rows // nd, D)
    every = (nf, nd, rows // nd, D)
    pieces = length // Q
    subs = block // Q
    bits = len(bits_of(nd))
    dma = pltpu.SemaphoreType.DMA
    ordered = lambda s: (steps - 1 - s, 0)
    ordered3 = lambda s: (steps - 1 - s, 0, 0)
    layer = 0 if last else 1
    conv_w, conv_b, dtb, alog, skip, gain = small
    return pl.pallas_call(
        functools.partial(layer_back_kernel, ch, nf, nd, last),
        grid=(steps,),
        in_specs=[
            pl.BlockSpec((block, D), ordered),
            pl.BlockSpec((block, width), ordered),
            pl.BlockSpec((block, conv_width), ordered),
            pl.BlockSpec((block, ch), ordered),
            pl.BlockSpec((subs, N, ch), ordered3),
            pl.BlockSpec((block, LANES), ordered),
            pl.BlockSpec((subs, 1, Q), ordered3),
            once((pieces, Q)),
            once((pieces, Q)),
        ]
        + [pick(part, layer) for part in (conv_w, dtb, alog, skip, gain)]
        + [
            pl.BlockSpec(memory_space=pl.ANY),
            pl.BlockSpec(memory_space=pl.ANY),
            once(own),
            once(own),
            pick(norm_gain, layer),
            once(own),
        ]
        + [pl.BlockSpec(memory_space=pl.ANY)] * (len(sums) + len(leaving)),
        out_specs=[
            pl.BlockSpec((block, width), ordered),
            once((16, conv_width)),
            once(own),
            once((pieces, Q)),
            pl.BlockSpec(memory_space=pl.ANY),
        ]
        + [pl.BlockSpec(memory_space=pl.ANY)] * (len(sums) + len(leaving)),
        out_shape=[
            jax.ShapeDtypeStruct((length, width), BF16),
            jax.ShapeDtypeStruct((16, conv_width), F32),
            jax.ShapeDtypeStruct(own, BF16),
            jax.ShapeDtypeStruct((pieces, Q), F32),
            jax.ShapeDtypeStruct((rows, D) if last else every, BF16),
        ]
        + [jax.ShapeDtypeStruct(shape, BF16) for shape in shapes]
        + [jax.ShapeDtypeStruct((rows, D), BF16) for part in leaving],
        scratch_shapes=[
            pltpu.VMEM(held_shape(w_in), BF16),
            pltpu.VMEM((ch, D), BF16),
            pltpu.VMEM((K - 1, Q + 8, conv_width), F32),
            pltpu.VMEM((N, ch), F32),
            pltpu.VMEM((block, ch), F32),
            pltpu.VMEM(every, BF16),
            pltpu.VMEM((bits, nf, nd // 2, rows // nd, D), BF16),
            pltpu.VMEM((nd, pieces, Q), F32),
            pltpu.VMEM(own, BF16),
            pltpu.VMEM((1, D), F32),
            dma((bits, nf, nd)),
            dma((bits, nf, nd)),
            dma((nd,)),
            dma((nd,)),
            dma((nf, nd)),
            dma((nf, nd)),
            dma((2 + nf,)),
            dma((nf,)),
            dma((nf,)),
            dma((nf,)),
        ]
        + [part for shape in shapes for part in section_sum_scratch(nf, shape)],
        compiler_params=pltpu.CompilerParams(
            vmem_limit_bytes=VMEM_LIMIT, collective_id=identity, has_side_effects=True
        ),
        name="layer_back_last" if last else "layer_back_first",
    )(
        grad_all, proj, pre, mixed, states, meta, segrow, ratio, pull, conv_w, dtb, alog, skip, gain, w_in, w_out,
        hidden, grad_own, norm_gain, branch, *sums, *leaving,
    )


def shards(
    inputs, segment, cotangent, norm_gain, in_weight, conv_weight, conv_bias, dt_bias, a_log, d_skip,
    gate_gain, out_weight,
):
    fsdp, dp = lax.axis_size("fsdp"), lax.axis_size("dp")
    section, here = lax.axis_index("section"), lax.axis_index("dp")
    rows = inputs.shape[2]
    ch = DI // dp
    heads = H // dp
    conv_width = ch + 2 * N
    seg_mine = lax.dynamic_index_in_dim(segment, section, 0, keepdims=False)[0].astype(F32)
    seg_mine = jnp.broadcast_to(seg_mine.reshape(rows // Q, 1, Q), (rows // Q, 8, Q)).reshape(-1, Q)
    head_table = jnp.pad(
        jnp.concatenate([dt_bias[0], a_log[0], d_skip[0]], axis=0), ((0, 0), (0, LANES - H))
    )
    (
        proj, mixed, pre, states, nout, branch, after, ratio, conv_w, conv_b, dtb, alog, skip, gain, gains, meta, segrow,
        normed_all, moved, hidden, cot_own, w_in0, w_in1, w_out0, w_out1,
    ) = run_first(
        ch, fsdp, dp, inputs[:, 0], cotangent[:, 0], seg_mine, in_weight[0, 0].T, out_weight[0, 0], conv_weight[0, 0],
        conv_bias[0], norm_gain[0], gate_gain[0], head_table, 2,
    )
    small = (conv_w, conv_b, dtb, alog, skip, gain)
    length = meta.shape[0]
    saved = [(normed_all.reshape(length, D), hidden, proj, nout, mixed, pre, states, branch, ratio)]
    normed_all, hidden = moved.reshape(length, D), after
    proj, nout, mixed, pre, states, branch, final_rows, ratio, pull, cot_all = run_layer(
        ch, rows, fsdp, dp, normed_all, meta, segrow, small, w_in1, w_out1, hidden, cot_own, 3
    )
    saved.append((normed_all, hidden, proj, nout, mixed, pre, states, branch, ratio))

    grad_all, grad_own = cot_all.reshape(length, D), cot_own
    in_grad, small_grads, parts = (), [None, None], []
    for layer in (1, 0):
        last = layer == 0
        normed_all, hidden, proj, gated, mixed, pre, states, branch, ratio = saved[layer]
        out_grad = dot(gated, grad_all, ((0,), (0,)))
        dproj, small_grads[layer], after, next_pull, moved, *done = run_layer_back(
            ch, rows, fsdp, dp, last, grad_all, proj, pre, mixed, states, meta, segrow, ratio, pull, small,
            w_in0 if last else w_in1, w_out0 if last else w_out1, hidden, grad_own, gains, saved[0][7], 4 + layer,
            (out_grad.astype(BF16),) + in_grad, *(() if last else (final_rows,)),
        )
        if not last:
            *done, final = done
        parts += done
        grad = dot(dproj, normed_all, ((0,), (0,))).astype(BF16)
        if D // fsdp % LANES:
            grad = jnp.swapaxes(grad.reshape(-1, fsdp, D // fsdp), 0, 1)
        in_grad = (grad,)
        if not last:
            grad_all, grad_own, pull = moved.reshape(length, D), after, next_pull
    input_grad = moved

    in_all, out_all, small_all = run_end(
        fsdp, dp, in_grad[0], parts[2], parts[1], parts[0], small_grads[0], small_grads[1]
    )
    in_total, out_total, gain_total, convw_total, convb_total, dtb_total, alog_total, skip_total, gate_total = run_finish(
        ch, dp, in_all, out_all, small_all
    )
    return (
        final[None, None],
        input_grad[None, None],
        gain_total[None],
        in_total.T[None, None],
        convw_total[None, None],
        convb_total[None],
        dtb_total[None],
        alog_total[None],
        skip_total[None],
        gate_total[None],
        out_total[None, None],
    )


def solution(mesh):
    return jax.shard_map(
        shards,
        mesh=mesh,
        in_specs=(
            P(None, "dp", "fsdp", None),
            P(None, "dp", "fsdp"),
            P(None, "dp", "fsdp", None),
            P("section", None, None),
            P("section", None, "fsdp", None),
            P("section", None, None, None),
            P("section", None, None),
            P("section", None, None),
            P("section", None, None),
            P("section", None, None),
            P("section", None, None),
            P("section", None, "fsdp", None),
        ),
        out_specs=(
            P("section", "dp", "fsdp", None),
            P("section", "dp", "fsdp", None),
            P("section", None, None),
            P("section", None, "fsdp", None),
            P("section", None, None, None),
            P("section", None, None),
            P("section", None, None),
            P("section", None, None),
            P("section", None, None),
            P("section", None, None),
            P("section", None, "fsdp", None),
        ),
        check_vma=False,
    )
```

profile of v0, /device:TPU:23, one launch (start us, length us, event | category | flops | bytes accessed | tf_op | source)
XLA Modules:
  0.0 711.2 jit_solution(13794541067163975797)
XLA Ops:
  0.6 0.7 dynamic-slice_convert_fusion
  1.3 1.3 select_maximum_fusion.head_ref
  2.6 0.6 broadcast_bitcast_fusion.seg_ref
  3.2 241.8 %layer_first.1 = (f32[1024,1840]{1,0:T(8,128)}, f32[1024,768]{1,0:T(8,128)}, f32[1024,1024]{1,0:T(8,128)}, f32[8,128,768]{2,1,0:T(8,128)}, bf16[1024,768]{1,0:T(...) custom-call(bf16[2,256,1536]{2,1,0:T(8,128)(2,1)} %bitcast.49, ...), custom_call_target="tpu_custom_call" | custom-call | tf_op jit(solution)/shard_map/layer_first/pallas_call | solution.py:1545
  245.0 87.4 %layer_last.1 = (f32[1024,1840]{1,0:T(8,128)}, bf16[1024,768]{1,0:T(8,128)(2,1)}, f32[1024,768]{1,0:T(8,128)}, f32[1024,1024]{1,0:T(8,128)}, f32[8,128,768]{2,1,...) custom-call(bf16[1024,1536]{1,0:T(8,128)(2,1)} %bitcast.46, ...), custom_call_target="tpu_custom_call" | custom-call | tf_op jit(solution)/shard_map/layer_last/pallas_call | solution.py:1760
  332.4 6.4 convolution_convert_fusion.3.refs_0_
  338.8 0.0 copy-start.5
  338.8 85.7 %layer_back_first.1 = (bf16[1024,1840]{1,0:T(8,128)(2,1)}, f32[16,1024]{1,0:T(8,128)}, bf16[4,64,1536]{2,1,0:T(8,128)(2,1)}, f32[8,128]{1,0:T(8,128)}, bf16[4,4,...) custom-call(bf16[1024,1536]{1,0:T(8,128)(2,1)} %bitcast.45, ...), custom_call_target="tpu_custom_call" | custom-call | tf_op jit(solution)/shard_map/layer_back_first/pallas_call | solution.py:2146
  424.5 0.0 copy-done.5
  424.5 0.0 copy-start
  424.5 0.0 copy-start.3
  424.5 5.9 convolution_convert_fusion.2.refs_0_
  430.5 0.0 copy-done
  430.5 0.0 copy-done.3
  430.5 8.0 %convolution_convert_fusion.1.refs_1_ = bf16[1840,1536]{1,0:T(8,128)(2,1)} fusion(bf16[1024,1840]{1,0:T(8,128)(2,1)S(1)} %copy-done.3, bf16[1024,1536]{1,0:T(8,128)(2,1)S(1)} %bitcast.47), kind=kOutput, calls=%fused_computation.1 | convolution fusion | flops 5790965760 | bytes 12566528 | tf_op jit(solution)/shard_map/dot_general | solution.py:27
  438.5 0.0 copy-start.4
  438.5 123.1 %layer_back_last.1 = (bf16[1024,1840]{1,0:T(8,128)(2,1)}, f32[16,1024]{1,0:T(8,128)}, bf16[4,64,1536]{2,1,0:T(8,128)(2,1)}, f32[8,128]{1,0:T(8,128)}, bf16[256,1...) custom-call(bf16[1024,1536]{1,0:T(8,128)(2,1)} %bitcast.43, ...), custom_call_target="tpu_custom_call" | custom-call | tf_op jit(solution)/shard_map/layer_back_last/pallas_call | solution.py:2146
  561.6 0.0 copy-done.4
  561.6 10.0 %convolution_convert_fusion.in_ref = bf16[1840,1536]{1,0:T(8,128)(2,1)} fusion(bf16[1024,1840]{1,0:T(8,128)(2,1)} %get-tuple-element.108, bf16[1024,1536]{1,0:T(8,128)(2,1)S(1)} %bitcast.63), kind=kOutput, calls=%fused_computation | convolution fusion | flops 5790965760 | bytes 12566528 | tf_op jit(solution)/shard_map/dot_general | solution.py:27
  571.7 126.3 %sum_end.1 = (bf16[4,1840,384]{2,1,0:T(8,128)(2,1)}, bf16[768,1536]{1,0:T(8,128)(2,1)}, f32[4,16,1024]{2,1,0:T(8,128)}) custom-call(bf16[1840,1536]{1,0:T(8,128)(2,1)} %convolution_convert_fusion.in_ref, bf16[928,384]{1,0:T(8,128)(2,1)} %get-tuple-element.110.in_part1_ref, bf16[192,768]{1,0:T(8,128)(2,1)} %get-tuple-element.111.out_part0_ref, ...), custom_call_target="tpu_custom_call" | custom-call | tf_op jit(solution)/shard_map/sum_end/pallas_call | solution.py:1002
  698.0 0.0 copy-start.1
  698.0 0.0 copy-start.2
  698.0 11.0 %finish.1 = (f32[6448,384]{1,0:T(8,128)}, f32[768,1536]{1,0:T(8,128)}, f32[1,1536]{1,0:T(1,128)}, f32[4,3328]{1,0:T(4,128)}, f32[1,3328]{1,0:T(1,128)}, /*index=...) custom-call(bf16[4,1840,384]{2,1,0:T(8,128)(2,1)} %get-tuple-element.115.in_ref.shared_ref, ...), custom_call_target="tpu_custom_call" | custom-call | tf_op jit(solution)/shard_map/finish/pallas_call | solution.py:1093
  709.0 0.0 copy-done.1
  709.0 0.9 copy.25
  709.9 0.0 copy-done.2
  709.9 0.9 copy.26
Async XLA Ops:
  338.8 85.7 %copy-start.5 = (bf16[1024,768]{1,0:T(8,128)(2,1)S(1)}, bf16[1024,768]{1,0:T(8,128)(2,1)}, u32[]{:S(2)}) copy-start(bf16[1024,768]{1,0:T(8,128)(2,1)} %get-tuple-element.105) | copy-start | bytes 4718596
  424.5 5.9 copy-start
  424.5 5.9 copy-start.3
  438.5 123.1 %copy-start.4 = (bf16[4,4,64,1536]{3,2,1,0:T(8,128)(2,1)S(1)}, bf16[4,4,64,1536]{3,2,1,0:T(8,128)(2,1)}, u32[]{:S(2)}) copy-start(bf16[4,4,64,1536]{3,2,1,0:T(8,128)(2,1)} %get-tuple-element.109) | copy-start | bytes 9437188
  698.0 11.0 %copy-start.1 = (bf16[256,1536]{1,0:T(8,128)(2,1)S(1)}, bf16[256,1536]{1,0:T(8,128)(2,1)}, u32[]{:S(2)}) copy-start(bf16[256,1536]{1,0:T(8,128)(2,1)} %get-tuple-element.93) | copy-start | bytes 2359300
  698.0 11.9 %copy-start.2 = (bf16[256,1536]{1,0:T(8,128)(2,1)S(1)}, bf16[256,1536]{1,0:T(8,128)(2,1)}, u32[]{:S(2)}) copy-start(bf16[256,1536]{1,0:T(8,128)(2,1)} %get-tuple-element.107) | copy-start | bytes 2359300
where the time goes:
time: 719 us; the launch traced here: 711 us
  Pallas kernels  675 us (94%)
  matrix products  30.4 us (4%)
    pallas_call x1, Pallas kernels, run_first(): pl.pallas_call(functools.partial(first_kernel, ch, nf, nd), grid=(nf,), i...  242 us
    pallas_call x2, Pallas kernels, run_layer_back(): pl.pallas_call(functools.partial(layer_back_kernel, ch, nf, nd, last), gr...  209 us
    pallas_call x1, Pallas kernels, run_end(): pl.pallas_call(functools.partial(end_kernel, nf, nd), in_specs=[anywhere]...  126 us
    pallas_call x1, Pallas kernels, run_layer(): pl.pallas_call(functools.partial(layer_kernel, ch, nf, nd), grid=(steps,)...  87.4 us
    dot_general x4, matrix products, dot(): lax.dot_general(a, b, (dims, ((), ())), preferred_element_type=F32, preci...  30.4 us

commit v1 on v0

--- a/solution.py
+++ b/solution.py
@@ -214,9 +214,12 @@
         self.bits = bits_of(peers)
         self.send_sem, self.recv_sem = send_sem, recv_sem
 
+    def slot(self, k, owner):
+        return self.peers - self.peers // self.bits[k] + owner // (2 * self.bits[k])
+
     def copy(self, k, block, owner):
         return remote(
-            self.partial.at[block, owner], self.landed.at[k, block, owner // 2], self.send_sem.at[k, block, owner],
+            self.partial.at[block, owner], self.landed.at[self.slot(k, owner), block], self.send_sem.at[k, block, owner],
             self.recv_sem.at[k, block, owner], {"dp": flip(self.here, self.bits[k])},
         )
 
@@ -224,7 +227,7 @@
         total = self.partial[block, owner].astype(F32)
         for m in range(stages):
             self.copy(m, block, owner).wait_recv()
-            total = total + self.landed[m, block, owner // 2].astype(F32)
+            total = total + self.landed[self.slot(m, owner), block].astype(F32)
         return total
 
     def leaving(self, k):
@@ -1586,7 +1589,7 @@
             pltpu.VMEM((N, ch), F32),
             pltpu.VMEM((2, block, ch), F32),
             pltpu.VMEM(every, F32),
-            pltpu.VMEM((bits, nf, nd // 2, block // nd, D), F32),
+            pltpu.VMEM((nd - 1, nf, block // nd, D), F32),
             pltpu.VMEM((nf, nd, 8, LANES), F32),
             pltpu.VMEM(own, BF16),
             pltpu.VMEM(every, BF16),
@@ -1803,7 +1806,7 @@
             pltpu.VMEM((N, ch), F32),
             pltpu.VMEM((2, block, ch), F32),
             pltpu.VMEM(every, BF16),
-            pltpu.VMEM((bits, nf, nd // 2, rows // nd, D), BF16),
+            pltpu.VMEM((nd - 1, nf, rows // nd, D), BF16),
             pltpu.VMEM((steps, nd, 8, LANES), F32),
             pltpu.VMEM((nd, pieces, Q), F32),
             dma((bits, nf, nd)),
@@ -1825,7 +1828,7 @@
 def mix_backward(
     ch, proj_ref, pre_ref, mixed_ref, state_ref, grad_ref, ratio_ref, pull_ref, meta_ref, segrow_ref,
     conv_w_ref, dtb_ref, alog_ref, skip_ref, gain_ref,
-    dproj_ref, small_ref, tail, dstate, sub, chunk, turn,
+    dproj_ref, small_ref, tail, work, dstate, sub, chunk, turn,
 ):
     conv_width = ch + 2 * N
     rows = pl.ds(pl.multiple_of(sub * Q, Q), Q)
@@ -1953,9 +1956,10 @@
     small_ref[3:4, :] += jnp.sum(raw * dpre, axis=0, keepdims=True)
     for lag in range(1, K):
         kept = meta[:, lag : lag + 1] * dpre
-        tail[lag - 1, 0:Q, :] = kept
-        moved = tail[lag - 1, lag : lag + Q, :]
-        tail[lag - 1, Q : Q + 8, :] = kept[0:8, :]
+        work[0:Q, :] = kept
+        work[Q : Q + 8, :] = tail[lag - 1]
+        moved = work[lag : lag + Q, :]
+        tail[lag - 1] = kept[0:8, :]
         draw = draw + conv_w_ref[3 - lag : 4 - lag, :] * moved
         small_ref[3 - lag : 4 - lag, :] += jnp.sum(raw * moved, axis=0, keepdims=True)
     dproj_ref[rows, ch : ch + conv_width] = draw.astype(BF16)
@@ -1966,15 +1970,17 @@
 
 
 def layer_back_kernel(
-    ch, nf, nd, last,
+    ch, nf, nd, last, fused,
     grad_all_ref, proj_ref, pre_ref, mixed_ref, state_ref, meta_ref, segrow_ref, ratio_ref, pull_ref,
     conv_w_ref, dtb_ref, alog_ref, skip_ref, gain_ref, w_in_ref, w_out_ref,
     hidden_ref, grad_own_ref, norm_gain_ref, branch_ref, *refs,
 ):
     count = 2 if last else 1
-    sources, refs = refs[:count], refs[count:]
+    sources, refs = refs[: count - fused], refs[count - fused :]
     if not last:
         rows_out, refs = refs[0], refs[1:]
+    if fused:
+        (normed_ref, nout_ref, grads_ref), refs = refs[:3], refs[3:]
     (
         dproj_ref, small_ref, next_ref, next_pull_ref, moved_ref,
     ) = refs[:5]
@@ -1982,10 +1988,21 @@
     if not last:
         final_ref, refs = refs[0], refs[1:]
     (
-        held, w_out, tail, dstate, dnout, partial, landed, pulls, low, dgain,
+        held, w_out, tail, work, dstate, dnout, partial, landed, pulls, low, dgain,
         sum_send, sum_recv, tile_send, tile_recv, group_send, group_recv, local_sem, load_sem, deal_send, deal_recv,
-    ) = refs[:20]
-    refs = refs[20:]
+    ) = refs[:21]
+    refs = refs[21:]
+    if fused:
+        dproj_all, normed, staged, out_grad, normed_sem, staged_sem = refs[-6:]
+        refs = refs[:-6]
+        nout = dproj_all.at[:, pl.ds(0, ch)]
+        block = grad_all_ref.shape[0]
+        weight_grad = dproj_ref
+        dproj_ref = dproj_all.at[pl.ds(pl.multiple_of((nf - 1 - pl.program_id(0)) * block, Q), block)]
+        normed_load = pltpu.make_async_copy(normed_ref, normed, normed_sem.at[0])
+        grads_load = pltpu.make_async_copy(grads_ref, normed, normed_sem.at[0])
+        nout_load = pltpu.make_async_copy(nout_ref, nout, normed_sem.at[1])
+        sources = (out_grad,) + sources
     step = pl.program_id(0)
     y, z, d = lax.axis_index("section"), lax.axis_index("fsdp"), lax.axis_index("dp")
     block = grad_all_ref.shape[0]
@@ -2021,7 +2038,10 @@
             + line_neighbours(nf, y, z)
             + deal_partners(nf, nd, z, d)
         )
-        for one in sums:
+        if fused:
+            grads_load.start()
+            nout_load.start()
+        for one in sums[::-1] if not fused else sums[:0:-1]:
             one.begin()
         if not last:
             leave.start_all()
@@ -2030,6 +2050,18 @@
         small_ref[...] = jnp.zeros_like(small_ref)
         dgain[...] = jnp.zeros_like(dgain)
         pulls[0] = jnp.zeros(pulls.shape[1:], F32)
+        if fused:
+            grads_load.wait()
+            nout_load.wait()
+
+            def out_tile(i, carry):
+                part = pl.ds(pl.multiple_of(i * LANES, LANES), LANES)
+                out_grad[part, :] = dot(nout[:, part], normed[...], ((0,), (0,))).astype(BF16)
+                return carry
+
+            lax.fori_loop(0, ch // LANES, out_tile, 0)
+            sums[0].begin()
+            normed_load.start()
         for copy in weights.copies():
             copy.wait()
         out_load.wait()
@@ -2049,10 +2081,10 @@
         )
         moved = (grad_own_ref[place].astype(F32) + dhidden).astype(BF16)
         low[place] = moved
-        next_ref[place] = moved
         if last:
             leave.start(place)
         else:
+            next_ref[place] = moved
             first = place * block + d * rows
             pulls[0, pl.ds(first // Q, 1), :] += to_row(
                 jnp.sum(moved.astype(F32) * branch_ref[place], axis=1, keepdims=True), first % Q
@@ -2071,7 +2103,7 @@
         mix_backward(
             ch, proj_ref, pre_ref, mixed_ref, state_ref, dnout, ratio_ref, pull_ref, meta_ref, segrow_ref,
             conv_w_ref, dtb_ref, alog_ref, skip_ref, gain_ref,
-            dproj_ref, small_ref, tail, dstate, sub, place * subs + sub, d * (H // nd),
+            dproj_ref, small_ref, tail, work, dstate, sub, place * subs + sub, d * (H // nd),
         )
 
         @pl.when((turn == 0) & (step >= 1))
@@ -2101,6 +2133,29 @@
     @pl.when(step == nf - 1)
     def _():
         pass_on(0)
+        if fused:
+            normed_load.wait()
+            width = dproj_all.shape[1]
+            wide = staged.shape[1]
+            full = width // wide
+
+            def store(i, size):
+                rows = pl.ds(pl.multiple_of(i * wide, 16), size)
+                return pltpu.make_async_copy(
+                    staged.at[i % 2, pl.ds(0, size)], weight_grad.at[rows], staged_sem.at[i % 2]
+                )
+
+            def some(i, carry):
+                @pl.when(i >= 2)
+                def _():
+                    store(i - 2, wide).wait()
+
+                columns = dproj_all[:, pl.ds(pl.multiple_of(i * wide, LANES), wide)]
+                staged[i % 2] = dot(columns, normed[...], ((0,), (0,))).astype(BF16)
+                store(i, wide).start()
+                return carry
+
+            lax.fori_loop(0, full // 2, some, 0)
         conclude(0)
         for row, (start, size) in enumerate(gain_rows(small_ref.shape[1])):
             small_ref[8 + row : 9 + row, 0:size] = dgain[:, start : start + size]
@@ -2108,6 +2163,15 @@
             next_pull_ref[...] = jnp.zeros_like(next_pull_ref)
         else:
             next_pull_ref[...] = group_tiles(pulls, tile_send, tile_recv, d, nd)
+        if fused:
+            lax.fori_loop(full // 2, full, some, 0)
+            store(full - 2, wide).wait()
+            rest = width - full * wide
+            if rest:
+                staged[full % 2, 0:rest] = dot(dproj_all[:, full * wide :], normed[...], ((0,), (0,))).astype(BF16)
+                store(full, rest).start()
+                store(full, rest).wait()
+            store(full - 1, wide).wait()
         for one, result in zip(sums, results):
             one.finish()
             copy = pltpu.make_async_copy(one.result, result, local_sem.at[1])
@@ -2126,10 +2190,13 @@
 
 def run_layer_back(
     ch, rows, nf, nd, last, grad_all, proj, pre, mixed, states, meta, segrow, ratio, pull, small, w_in, w_out,
-    hidden, grad_own, norm_gain, branch, identity, sums, *leaving,
+    hidden, grad_own, norm_gain, branch, identity, sums, leaving, more,
 ):
     length, width = proj.shape
-    shapes = [make(nf, g) for make, g in zip((out_part_shape, in_part_shape), sums)]
+    if more:
+        shapes = [out_part_shape(nf, w_out)] + [in_part_shape(nf, g) for g in sums]
+    else:
+        shapes = [make(nf, g) for make, g in zip((out_part_shape, in_part_shape), sums)]
     conv_width = ch + 2 * N
     block = rows
     steps = nf
@@ -2144,7 +2211,7 @@
     layer = 0 if last else 1
     conv_w, conv_b, dtb, alog, skip, gain = small
     return pl.pallas_call(
-        functools.partial(layer_back_kernel, ch, nf, nd, last),
+        functools.partial(layer_back_kernel, ch, nf, nd, last, bool(more)),
         grid=(steps,),
         in_specs=[
             pl.BlockSpec((block, D), ordered),
@@ -2164,19 +2231,19 @@
             once(own),
             once(own),
             pick(norm_gain, layer),
-            once(own),
+            pl.BlockSpec(memory_space=pl.ANY) if last else once(own),
         ]
-        + [pl.BlockSpec(memory_space=pl.ANY)] * (len(sums) + len(leaving)),
+        + [pl.BlockSpec(memory_space=pl.ANY)] * (len(sums) + len(leaving) + len(more)),
         out_specs=[
-            pl.BlockSpec((block, width), ordered),
+            pl.BlockSpec(memory_space=pl.ANY) if more else pl.BlockSpec((block, width), ordered),
             once((16, conv_width)),
-            once(own),
+            pl.BlockSpec(memory_space=pl.ANY) if last else once(own),
             once((pieces, Q)),
             pl.BlockSpec(memory_space=pl.ANY),
         ]
-        + [pl.BlockSpec(memory_space=pl.ANY)] * (len(sums) + len(leaving)),
+        + [pl.BlockSpec(memory_space=pl.ANY)] * (len(shapes) + len(leaving)),
         out_shape=[
-            jax.ShapeDtypeStruct((length, width), BF16),
+            jax.ShapeDtypeStruct((width, D) if more else (length, width), BF16),
             jax.ShapeDtypeStruct((16, conv_width), F32),
             jax.ShapeDtypeStruct(own, BF16),
             jax.ShapeDtypeStruct((pieces, Q), F32),
@@ -2187,11 +2254,12 @@
         scratch_shapes=[
             pltpu.VMEM(held_shape(w_in), BF16),
             pltpu.VMEM((ch, D), BF16),
-            pltpu.VMEM((K - 1, Q + 8, conv_width), F32),
+            pltpu.VMEM((K - 1, 8, conv_width), F32),
+            pltpu.VMEM((Q + 8, conv_width), F32),
             pltpu.VMEM((N, ch), F32),
             pltpu.VMEM((block, ch), F32),
             pltpu.VMEM(every, BF16),
-            pltpu.VMEM((bits, nf, nd // 2, rows // nd, D), BF16),
+            pltpu.VMEM((nd - 1, nf, rows // nd, D), BF16),
             pltpu.VMEM((nd, pieces, Q), F32),
             pltpu.VMEM(own, BF16),
             pltpu.VMEM((1, D), F32),
@@ -2206,14 +2274,26 @@
             dma((nf,)),
             dma((nf,)),
         ]
-        + [part for shape in shapes for part in section_sum_scratch(nf, shape)],
+        + [part for shape in shapes for part in section_sum_scratch(nf, shape)]
+        + (
+            [
+                pltpu.VMEM((length, width), BF16),
+                pltpu.VMEM((length, D), BF16),
+                pltpu.VMEM((2, LANES, D), BF16),
+                pltpu.VMEM((ch, D), BF16),
+                dma((2,)),
+                dma((2,)),
+            ]
+            if more
+            else []
+        ),
         compiler_params=pltpu.CompilerParams(
             vmem_limit_bytes=VMEM_LIMIT, collective_id=identity, has_side_effects=True
         ),
         name="layer_back_last" if last else "layer_back_first",
     )(
         grad_all, proj, pre, mixed, states, meta, segrow, ratio, pull, conv_w, dtb, alog, skip, gain, w_in, w_out,
-        hidden, grad_own, norm_gain, branch, *sums, *leaving,
+        hidden, grad_own, norm_gain, branch, *sums, *leaving, *more,
     )
 
 
@@ -2250,20 +2330,24 @@
 
     grad_all, grad_own = cot_all.reshape(length, D), cot_own
     in_grad, small_grads, parts = (), [None, None], []
+    fused = D // fsdp % LANES == 0
     for layer in (1, 0):
         last = layer == 0
         normed_all, hidden, proj, gated, mixed, pre, states, branch, ratio = saved[layer]
-        out_grad = dot(gated, grad_all, ((0,), (0,)))
+        out_grad = () if fused else (dot(gated, grad_all, ((0,), (0,))).astype(BF16),)
         dproj, small_grads[layer], after, next_pull, moved, *done = run_layer_back(
             ch, rows, fsdp, dp, last, grad_all, proj, pre, mixed, states, meta, segrow, ratio, pull, small,
             w_in0 if last else w_in1, w_out0 if last else w_out1, hidden, grad_own, gains, saved[0][7], 4 + layer,
-            (out_grad.astype(BF16),) + in_grad, *(() if last else (final_rows,)),
+            out_grad + in_grad, () if last else (final_rows,), (normed_all, gated, grad_all) if fused else (),
         )
         if not last:
             *done, final = done
         parts += done
-        grad = dot(dproj, normed_all, ((0,), (0,))).astype(BF16)
-        if D // fsdp % LANES:
+        if fused:
+            grad = dproj
+        else:
+            grad = dot(dproj, normed_all, ((0,), (0,))).astype(BF16)
+        if not fused:
             grad = jnp.swapaxes(grad.reshape(-1, fsdp, D // fsdp), 0, 1)
         in_grad = (grad,)
         if not last:

time: 719 us -> 705 us (0.981)
  matrix products: 30.4 us -> 0 us
  Pallas kernels: 675 us -> 692 us
    dot_general x4 -> x0, matrix products: 30.4 us -> none  [dot(): lax.dot_general(a, b, (dims, ((), ())), preferred_element_type=F32, preci...]
    pallas_call x2, Pallas kernels: 209 us -> 221 us  [run_layer_back(): pl.pallas_call(functools.partial(layer_back_kernel, ch, nf, nd, last, boo...]
    pallas_call x1, Pallas kernels: 87.4 us -> 97.5 us  [run_layer(): pl.pallas_call(functools.partial(layer_kernel, ch, nf, nd), grid=(steps,)...]
where the time goes in v1:
time: 705 us; the launch traced here: 697 us
  Pallas kernels  692 us (98%)
    pallas_call x1, Pallas kernels, run_first(): pl.pallas_call(functools.partial(first_kernel, ch, nf, nd), grid=(nf,), i...  242 us
    pallas_call x2, Pallas kernels, run_layer_back(): pl.pallas_call(functools.partial(layer_back_kernel, ch, nf, nd, last, boo...  221 us
    pallas_call x1, Pallas kernels, run_end(): pl.pallas_call(functools.partial(end_kernel, nf, nd), in_specs=[anywhere]...  121 us
    pallas_call x1, Pallas kernels, run_layer(): pl.pallas_call(functools.partial(layer_kernel, ch, nf, nd), grid=(steps,)...  97.5 us

profile of v1, /device:TPU:23, one launch (start us, length us, event | category | flops | bytes accessed | tf_op | source)
XLA Modules:
  0.0 697.3 jit_solution(5138385201811008807)
XLA Ops:
  0.6 0.7 dynamic-slice_convert_fusion
  1.3 1.3 select_maximum_fusion.head_ref
  2.6 0.6 broadcast_bitcast_fusion.seg_ref
  3.2 241.8 %layer_first.1 = (f32[1024,1840]{1,0:T(8,128)}, f32[1024,768]{1,0:T(8,128)}, f32[1024,1024]{1,0:T(8,128)}, f32[8,128,768]{2,1,0:T(8,128)}, bf16[1024,768]{1,0:T(...) custom-call(bf16[2,256,1536]{2,1,0:T(8,128)(2,1)} %bitcast.42, ...), custom_call_target="tpu_custom_call" | custom-call | tf_op jit(solution)/shard_map/layer_first/pallas_call | solution.py:1548
  245.0 97.5 %layer_last.1 = (f32[1024,1840]{1,0:T(8,128)}, bf16[1024,768]{1,0:T(8,128)(2,1)}, f32[1024,768]{1,0:T(8,128)}, f32[1024,1024]{1,0:T(8,128)}, f32[8,128,768]{2,1,...) custom-call(bf16[1024,1536]{1,0:T(8,128)(2,1)} %bitcast.35, ...), custom_call_target="tpu_custom_call" | custom-call | tf_op jit(solution)/shard_map/layer_last/pallas_call | solution.py:1763
  342.4 94.1 %layer_back_first.1 = (bf16[1840,1536]{1,0:T(8,128)(2,1)}, f32[16,1024]{1,0:T(8,128)}, bf16[4,64,1536]{2,1,0:T(8,128)(2,1)}, f32[8,128]{1,0:T(8,128)}, bf16[4,4,...) custom-call(bf16[1024,1536]{1,0:T(8,128)(2,1)} %bitcast.33, ...), custom_call_target="tpu_custom_call" | custom-call | tf_op jit(solution)/shard_map/layer_back_first/pallas_call | solution.py:2213
  436.5 126.6 %layer_back_last.1 = (bf16[1840,1536]{1,0:T(8,128)(2,1)}, f32[16,1024]{1,0:T(8,128)}, bf16[4,64,1536]{2,1,0:T(8,128)(2,1)}, f32[8,128]{1,0:T(8,128)}, bf16[256,1...) custom-call(bf16[1024,1536]{1,0:T(8,128)(2,1)} %bitcast.37, ...), custom_call_target="tpu_custom_call" | custom-call | tf_op jit(solution)/shard_map/layer_back_last/pallas_call | solution.py:2213
  563.1 121.4 %sum_end.1 = (bf16[4,1840,384]{2,1,0:T(8,128)(2,1)}, bf16[768,1536]{1,0:T(8,128)(2,1)}, f32[4,16,1024]{2,1,0:T(8,128)}) custom-call(bf16[1840,1536]{1,0:T(8,128)(2,1)} %get-tuple-element.109.in_ref, bf16[928,384]{1,0:T(8,128)(2,1)} %get-tuple-element.110.in_part1_ref, bf16[192,768]{1,0:T(8,128)(2,1)} %get-tuple-element.111.out_part0_ref, ...), custom_call_target="tpu_custom_call" | custom-call | tf_op jit(solution)/shard_map/sum_end/pallas_call | solution.py:1005
  684.5 0.0 copy-start
  684.5 0.0 copy-start.1
  684.6 11.0 %finish.1 = (f32[6448,384]{1,0:T(8,128)}, f32[768,1536]{1,0:T(8,128)}, f32[1,1536]{1,0:T(1,128)}, f32[4,3328]{1,0:T(4,128)}, f32[1,3328]{1,0:T(1,128)}, /*index=...) custom-call(bf16[4,1840,384]{2,1,0:T(8,128)(2,1)} %get-tuple-element.115.in_ref.shared_ref, ...), custom_call_target="tpu_custom_call" | custom-call | tf_op jit(solution)/shard_map/finish/pallas_call | solution.py:1096
  695.5 0.0 copy-done
  695.5 0.9 copy.25
  696.4 0.0 copy-done.1
  696.4 0.9 copy.26
Async XLA Ops:
  684.5 11.0 %copy-start = (bf16[256,1536]{1,0:T(8,128)(2,1)S(1)}, bf16[256,1536]{1,0:T(8,128)(2,1)}, u32[]{:S(2)}) copy-start(bf16[256,1536]{1,0:T(8,128)(2,1)} %get-tuple-element.93) | copy-start | bytes 2359300
  684.5 11.9 %copy-start.1 = (bf16[256,1536]{1,0:T(8,128)(2,1)S(1)}, bf16[256,1536]{1,0:T(8,128)(2,1)}, u32[]{:S(2)}) copy-start(bf16[256,1536]{1,0:T(8,128)(2,1)} %get-tuple-element.108) | copy-start | bytes 2359300

commit v2 on v1

--- a/solution.py
+++ b/solution.py
@@ -1162,11 +1162,16 @@
     conv_width = ch + 2 * N
     rows = pl.ds(pl.multiple_of(sub * Q, Q), Q)
     meta = meta_ref[rows, :]
-    pad[8:, :] = proj_ref[rows, ch : ch + conv_width]
-    pre = conv_b_ref[...] + conv_w_ref[3:4, :] * pad[8:, :]
+    raw = proj_ref[rows, ch : ch + conv_width]
+    pre = conv_b_ref[...] + conv_w_ref[3:4, :] * raw
+    before = pad[...]
+    first_rows = lax.broadcasted_iota(jnp.int32, (8, conv_width), 0)
     for lag in range(1, K):
-        pre = pre + (conv_w_ref[3 - lag : 4 - lag, :] * meta[:, lag : lag + 1]) * pad[8 - lag : 8 - lag + Q, :]
-    pad[0:8, :] = pad[Q : Q + 8, :]
+        earlier = pltpu.roll(raw, lag, 0)
+        begin = jnp.where(first_rows >= lag, earlier[0:8, :], pltpu.roll(before, lag, 0))
+        shifted = jnp.concatenate([begin, earlier[8:, :]], axis=0)
+        pre = pre + (conv_w_ref[3 - lag : 4 - lag, :] * meta[:, lag : lag + 1]) * shifted
+    pad[...] = raw[Q - 8 :, :]
     pre_ref[rows, :] = pre
     conv_out = pre * jax.nn.sigmoid(pre)
     values = conv_out[:, :ch]
@@ -1392,7 +1397,7 @@
         gathers[1].begin()
         first_group.finish()
         normed_copy.start()
-        pad[0:8, :] = jnp.zeros((8, pad.shape[1]), F32)
+        pad[...] = jnp.zeros_like(pad)
         state[...] = jnp.zeros_like(state)
         for k in range(1, nf):
             gathers[0].settle(k)
@@ -1585,7 +1590,7 @@
         scratch_shapes=[
             pltpu.VMEM(held_shape(w_in), BF16),
             pltpu.VMEM((ch, D), BF16),
-            pltpu.VMEM((Q + 8, conv_width), F32),
+            pltpu.VMEM((8, conv_width), F32),
             pltpu.VMEM((N, ch), F32),
             pltpu.VMEM((2, block, ch), F32),
             pltpu.VMEM(every, F32),
@@ -1653,7 +1658,7 @@
         greet([(None, {"dp": flip(d, j)}) for j in range(1, nd)])
         cot_keep.start()
         cot_group.begin(extra_ref)
-        pad[0:8, :] = jnp.zeros((8, pad.shape[1]), F32)
+        pad[...] = jnp.zeros_like(pad)
         state[...] = jnp.zeros_like(state)
         pulls[0] = jnp.zeros(pulls.shape[1:], F32)
         for copy in weights.copies():
@@ -1802,7 +1807,7 @@
         scratch_shapes=[
             pltpu.VMEM(held_shape(w_in), BF16),
             pltpu.VMEM((ch, D), BF16),
-            pltpu.VMEM((Q + 8, conv_width), F32),
+            pltpu.VMEM((8, conv_width), F32),
             pltpu.VMEM((N, ch), F32),
             pltpu.VMEM((2, block, ch), F32),
             pltpu.VMEM(every, BF16),
@@ -1828,7 +1833,7 @@
 def mix_backward(
     ch, proj_ref, pre_ref, mixed_ref, state_ref, grad_ref, ratio_ref, pull_ref, meta_ref, segrow_ref,
     conv_w_ref, dtb_ref, alog_ref, skip_ref, gain_ref,
-    dproj_ref, small_ref, tail, work, dstate, sub, chunk, turn,
+    dproj_ref, small_ref, tail, dstate, sub, chunk, turn,
 ):
     conv_width = ch + 2 * N
     rows = pl.ds(pl.multiple_of(sub * Q, Q), Q)
@@ -1953,12 +1958,13 @@
     raw = proj_ref[rows, ch : ch + conv_width]
     small_ref[4:5, :] += jnp.sum(dpre, axis=0, keepdims=True)
     draw = conv_w_ref[3:4, :] * dpre
+    last_rows = lax.broadcasted_iota(jnp.int32, (8, conv_width), 0)
     small_ref[3:4, :] += jnp.sum(raw * dpre, axis=0, keepdims=True)
     for lag in range(1, K):
         kept = meta[:, lag : lag + 1] * dpre
-        work[0:Q, :] = kept
-        work[Q : Q + 8, :] = tail[lag - 1]
-        moved = work[lag : lag + Q, :]
+        later = pltpu.roll(kept, Q - lag, 0)
+        end = jnp.where(last_rows < 8 - lag, later[Q - 8 :, :], pltpu.roll(tail[lag - 1], 8 - lag, 0))
+        moved = jnp.concatenate([later[: Q - 8, :], end], axis=0)
         tail[lag - 1] = kept[0:8, :]
         draw = draw + conv_w_ref[3 - lag : 4 - lag, :] * moved
         small_ref[3 - lag : 4 - lag, :] += jnp.sum(raw * moved, axis=0, keepdims=True)
@@ -1988,10 +1994,10 @@
     if not last:
         final_ref, refs = refs[0], refs[1:]
     (
-        held, w_out, tail, work, dstate, dnout, partial, landed, pulls, low, dgain,
+        held, w_out, tail, dstate, dnout, partial, landed, pulls, low, dgain,
         sum_send, sum_recv, tile_send, tile_recv, group_send, group_recv, local_sem, load_sem, deal_send, deal_recv,
-    ) = refs[:21]
-    refs = refs[21:]
+    ) = refs[:20]
+    refs = refs[20:]
     if fused:
         dproj_all, normed, staged, out_grad, normed_sem, staged_sem = refs[-6:]
         refs = refs[:-6]
@@ -2103,7 +2109,7 @@
         mix_backward(
             ch, proj_ref, pre_ref, mixed_ref, state_ref, dnout, ratio_ref, pull_ref, meta_ref, segrow_ref,
             conv_w_ref, dtb_ref, alog_ref, skip_ref, gain_ref,
-            dproj_ref, small_ref, tail, work, dstate, sub, place * subs + sub, d * (H // nd),
+            dproj_ref, small_ref, tail, dstate, sub, place * subs + sub, d * (H // nd),
         )
 
         @pl.when((turn == 0) & (step >= 1))
@@ -2255,7 +2261,6 @@
             pltpu.VMEM(held_shape(w_in), BF16),
             pltpu.VMEM((ch, D), BF16),
             pltpu.VMEM((K - 1, 8, conv_width), F32),
-            pltpu.VMEM((Q + 8, conv_width), F32),
             pltpu.VMEM((N, ch), F32),
             pltpu.VMEM((block, ch), F32),
             pltpu.VMEM(every, BF16),

time: 705 us -> 687 us (0.974)
  Pallas kernels: 692 us -> 681 us
    pallas_call x1, Pallas kernels: 97.5 us -> 87.3 us  [run_layer(): pl.pallas_call(functools.partial(layer_kernel, ch, nf, nd), grid=(steps,)...]
where the time goes in v2:
time: 687 us; the launch traced here: 686 us
  Pallas kernels  681 us (99%)
    pallas_call x1, Pallas kernels, run_first(): pl.pallas_call(functools.partial(first_kernel, ch, nf, nd), grid=(nf,), i...  242 us
    pallas_call x2, Pallas kernels, run_layer_back(): pl.pallas_call(functools.partial(layer_back_kernel, ch, nf, nd, last, boo...  219 us
    pallas_call x1, Pallas kernels, run_end(): pl.pallas_call(functools.partial(end_kernel, nf, nd), in_specs=[anywhere]...  122 us
    pallas_call x1, Pallas kernels, run_layer(): pl.pallas_call(functools.partial(layer_kernel, ch, nf, nd), grid=(steps,)...  87.3 us

profile of v2, /device:TPU:23, one launch (start us, length us, event | category | flops | bytes accessed | tf_op | source)
XLA Modules:
  0.0 685.9 jit_solution(3712844359730176090)
XLA Ops:
  0.6 0.7 dynamic-slice_convert_fusion
  1.3 1.3 select_maximum_fusion.head_ref
  2.6 0.6 broadcast_bitcast_fusion.seg_ref
  3.2 241.8 %layer_first.1 = (f32[1024,1840]{1,0:T(8,128)}, f32[1024,768]{1,0:T(8,128)}, f32[1024,1024]{1,0:T(8,128)}, f32[8,128,768]{2,1,0:T(8,128)}, bf16[1024,768]{1,0:T(...) custom-call(bf16[2,256,1536]{2,1,0:T(8,128)(2,1)} %bitcast.42, ...), custom_call_target="tpu_custom_call" | custom-call | tf_op jit(solution)/shard_map/layer_first/pallas_call | solution.py:1553
  245.0 87.3 %layer_last.1 = (f32[1024,1840]{1,0:T(8,128)}, bf16[1024,768]{1,0:T(8,128)(2,1)}, f32[1024,768]{1,0:T(8,128)}, f32[1024,1024]{1,0:T(8,128)}, f32[8,128,768]{2,1,...) custom-call(bf16[1024,1536]{1,0:T(8,128)(2,1)} %bitcast.35, ...), custom_call_target="tpu_custom_call" | custom-call | tf_op jit(solution)/shard_map/layer_last/pallas_call | solution.py:1768
  332.3 93.7 %layer_back_first.1 = (bf16[1840,1536]{1,0:T(8,128)(2,1)}, f32[16,1024]{1,0:T(8,128)}, bf16[4,64,1536]{2,1,0:T(8,128)(2,1)}, f32[8,128]{1,0:T(8,128)}, bf16[4,4,...) custom-call(bf16[1024,1536]{1,0:T(8,128)(2,1)} %bitcast.33, ...), custom_call_target="tpu_custom_call" | custom-call | tf_op jit(solution)/shard_map/layer_back_first/pallas_call | solution.py:2219
  426.0 125.4 %layer_back_last.1 = (bf16[1840,1536]{1,0:T(8,128)(2,1)}, f32[16,1024]{1,0:T(8,128)}, bf16[4,64,1536]{2,1,0:T(8,128)(2,1)}, f32[8,128]{1,0:T(8,128)}, bf16[256,1...) custom-call(bf16[1024,1536]{1,0:T(8,128)(2,1)} %bitcast.37, ...), custom_call_target="tpu_custom_call" | custom-call | tf_op jit(solution)/shard_map/layer_back_last/pallas_call | solution.py:2219
  551.5 121.6 %sum_end.1 = (bf16[4,1840,384]{2,1,0:T(8,128)(2,1)}, bf16[768,1536]{1,0:T(8,128)(2,1)}, f32[4,16,1024]{2,1,0:T(8,128)}) custom-call(bf16[1840,1536]{1,0:T(8,128)(2,1)} %get-tuple-element.109.in_ref, bf16[928,384]{1,0:T(8,128)(2,1)} %get-tuple-element.110.in_part1_ref, bf16[192,768]{1,0:T(8,128)(2,1)} %get-tuple-element.111.out_part0_ref, ...), custom_call_target="tpu_custom_call" | custom-call | tf_op jit(solution)/shard_map/sum_end/pallas_call | solution.py:1005
  673.1 0.0 copy-start
  673.1 0.0 copy-start.1
  673.1 11.0 %finish.1 = (f32[6448,384]{1,0:T(8,128)}, f32[768,1536]{1,0:T(8,128)}, f32[1,1536]{1,0:T(1,128)}, f32[4,3328]{1,0:T(4,128)}, f32[1,3328]{1,0:T(1,128)}, /*index=...) custom-call(bf16[4,1840,384]{2,1,0:T(8,128)(2,1)} %get-tuple-element.115.in_ref.shared_ref, ...), custom_call_target="tpu_custom_call" | custom-call | tf_op jit(solution)/shard_map/finish/pallas_call | solution.py:1096
  684.1 0.0 copy-done
  684.1 0.9 copy.25
  685.0 0.0 copy-done.1
  685.0 0.9 copy.26
Async XLA Ops:
  673.1 11.0 %copy-start = (bf16[256,1536]{1,0:T(8,128)(2,1)S(1)}, bf16[256,1536]{1,0:T(8,128)(2,1)}, u32[]{:S(2)}) copy-start(bf16[256,1536]{1,0:T(8,128)(2,1)} %get-tuple-element.93) | copy-start | bytes 2359300
  673.1 11.9 %copy-start.1 = (bf16[256,1536]{1,0:T(8,128)(2,1)S(1)}, bf16[256,1536]{1,0:T(8,128)(2,1)}, u32[]{:S(2)}) copy-start(bf16[256,1536]{1,0:T(8,128)(2,1)} %get-tuple-element.108) | copy-start | bytes 2359300

commit v3 on v2

--- a/solution.py
+++ b/solution.py
@@ -362,10 +362,10 @@
         )
 
     def right(self, k, b, part, source=None):
-        return self.send(b, part, 0, k, 2, {"fsdp": self.z + 1}, source)
+        return self.send(b, part, 0, k, 2, {"fsdp": (self.z + 1) % self.nf}, source)
 
     def left(self, k, b, part, source=None):
-        return self.send(b, part, 1, k, 3, {"fsdp": self.z - 1}, source)
+        return self.send(b, part, 1, k, 3, {"fsdp": (self.z + self.nf - 1) % self.nf}, source)
 
     def over(self, k, b, part, source=None):
         return self.send(b, part, 4, k, 5, self.peer, source)
@@ -521,10 +521,10 @@
         )
 
     def right(self, i, part, source=None):
-        return self.send(i, part, 0, 2, {"fsdp": self.z + 1}, source)
+        return self.send(i, part, 0, 2, {"fsdp": (self.z + 1) % self.nf}, source)
 
     def left(self, i, part, source=None):
-        return self.send(i, part, 1, 2, {"fsdp": self.z - 1}, source)
+        return self.send(i, part, 1, 2, {"fsdp": (self.z + self.nf - 1) % self.nf}, source)
 
     def over(self, i, part, source=None):
         return self.send(i, part, 3, 4, self.peer, source)
@@ -655,14 +655,14 @@
     def right(self, block):
         return remote(
             self.own.at[block], self.chain.at[block], self.chain_send.at[block], self.chain_recv.at[block],
-            {"fsdp": self.z + 1},
+            {"fsdp": (self.z + 1) % self.nf},
         )
 
     def left(self, block, arrives):
         slot = self.nf if arrives else block
         return remote(
             self.own.at[block], self.chain.at[slot], self.chain_send.at[block], self.chain_recv.at[slot],
-            {"fsdp": self.z - 1},
+            {"fsdp": (self.z + self.nf - 1) % self.nf},
         )
 
     def at(self, k, body):

time: 687 us -> 687 us (level)
  no operation moved by 1% of the time
where the time goes in v3:
time: 687 us; the launch traced here: 686 us
  Pallas kernels  680 us (99%)
    pallas_call x1, Pallas kernels, run_first(): pl.pallas_call(functools.partial(first_kernel, ch, nf, nd), grid=(nf,), i...  242 us
    pallas_call x2, Pallas kernels, run_layer_back(): pl.pallas_call(functools.partial(layer_back_kernel, ch, nf, nd, last, boo...  219 us
    pallas_call x1, Pallas kernels, run_end(): pl.pallas_call(functools.partial(end_kernel, nf, nd), in_specs=[anywhere]...  121 us
    pallas_call x1, Pallas kernels, run_layer(): pl.pallas_call(functools.partial(layer_kernel, ch, nf, nd), grid=(steps,)...  87.4 us

profile of v3, /device:TPU:23, one launch (start us, length us, event | category | flops | bytes accessed | tf_op | source)
XLA Modules:
  0.0 685.5 jit_solution(13589490137790899172)
XLA Ops:
  0.6 0.7 dynamic-slice_convert_fusion
  1.3 1.3 select_maximum_fusion.head_ref
  2.6 0.6 broadcast_bitcast_fusion.seg_ref
  3.2 241.8 %layer_first.1 = (f32[1024,1840]{1,0:T(8,128)}, f32[1024,768]{1,0:T(8,128)}, f32[1024,1024]{1,0:T(8,128)}, f32[8,128,768]{2,1,0:T(8,128)}, bf16[1024,768]{1,0:T(...) custom-call(bf16[2,256,1536]{2,1,0:T(8,128)(2,1)} %bitcast.42, ...), custom_call_target="tpu_custom_call" | custom-call | tf_op jit(solution)/shard_map/layer_first/pallas_call | solution.py:1553
  245.0 87.4 %layer_last.1 = (f32[1024,1840]{1,0:T(8,128)}, bf16[1024,768]{1,0:T(8,128)(2,1)}, f32[1024,768]{1,0:T(8,128)}, f32[1024,1024]{1,0:T(8,128)}, f32[8,128,768]{2,1,...) custom-call(bf16[1024,1536]{1,0:T(8,128)(2,1)} %bitcast.35, ...), custom_call_target="tpu_custom_call" | custom-call | tf_op jit(solution)/shard_map/layer_last/pallas_call | solution.py:1768
  332.4 93.5 %layer_back_first.1 = (bf16[1840,1536]{1,0:T(8,128)(2,1)}, f32[16,1024]{1,0:T(8,128)}, bf16[4,64,1536]{2,1,0:T(8,128)(2,1)}, f32[8,128]{1,0:T(8,128)}, bf16[4,4,...) custom-call(bf16[1024,1536]{1,0:T(8,128)(2,1)} %bitcast.33, ...), custom_call_target="tpu_custom_call" | custom-call | tf_op jit(solution)/shard_map/layer_back_first/pallas_call | solution.py:2219
  425.9 125.3 %layer_back_last.1 = (bf16[1840,1536]{1,0:T(8,128)(2,1)}, f32[16,1024]{1,0:T(8,128)}, bf16[4,64,1536]{2,1,0:T(8,128)(2,1)}, f32[8,128]{1,0:T(8,128)}, bf16[256,1...) custom-call(bf16[1024,1536]{1,0:T(8,128)(2,1)} %bitcast.37, ...), custom_call_target="tpu_custom_call" | custom-call | tf_op jit(solution)/shard_map/layer_back_last/pallas_call | solution.py:2219
  551.2 121.5 %sum_end.1 = (bf16[4,1840,384]{2,1,0:T(8,128)(2,1)}, bf16[768,1536]{1,0:T(8,128)(2,1)}, f32[4,16,1024]{2,1,0:T(8,128)}) custom-call(bf16[1840,1536]{1,0:T(8,128)(2,1)} %get-tuple-element.109.in_ref, bf16[928,384]{1,0:T(8,128)(2,1)} %get-tuple-element.110.in_part1_ref, bf16[192,768]{1,0:T(8,128)(2,1)} %get-tuple-element.111.out_part0_ref, ...), custom_call_target="tpu_custom_call" | custom-call | tf_op jit(solution)/shard_map/sum_end/pallas_call | solution.py:1005
  672.7 0.0 copy-start
  672.8 0.0 copy-start.1
  672.8 11.0 %finish.1 = (f32[6448,384]{1,0:T(8,128)}, f32[768,1536]{1,0:T(8,128)}, f32[1,1536]{1,0:T(1,128)}, f32[4,3328]{1,0:T(4,128)}, f32[1,3328]{1,0:T(1,128)}, /*index=...) custom-call(bf16[4,1840,384]{2,1,0:T(8,128)(2,1)} %get-tuple-element.115.in_ref.shared_ref, ...), custom_call_target="tpu_custom_call" | custom-call | tf_op jit(solution)/shard_map/finish/pallas_call | solution.py:1096
  683.7 0.0 copy-done
  683.7 0.9 copy.25
  684.6 0.0 copy-done.1
  684.6 0.9 copy.26
Async XLA Ops:
  672.7 11.0 %copy-start = (bf16[256,1536]{1,0:T(8,128)(2,1)S(1)}, bf16[256,1536]{1,0:T(8,128)(2,1)}, u32[]{:S(2)}) copy-start(bf16[256,1536]{1,0:T(8,128)(2,1)} %get-tuple-element.93) | copy-start | bytes 2359300
  672.8 11.9 %copy-start.1 = (bf16[256,1536]{1,0:T(8,128)(2,1)S(1)}, bf16[256,1536]{1,0:T(8,128)(2,1)}, u32[]{:S(2)}) copy-start(bf16[256,1536]{1,0:T(8,128)(2,1)} %get-tuple-element.108) | copy-start | bytes 2359300
